TPU v7x, 32 devices: a whole 2x2x4 slice. The times are simulated.
32 devices in a mesh: fine: 8 (over z, y), tele: 4 (over x, core).
Axes of the slice: x: 2, y: 2, z: 4, core: 2. Of those that a mesh axis runs over, the one named last changes fastest.
Arguments:
- right_side: float32 [512, 320], P(('fine', 'tele')), may hold values from -6 to 6
- fine_inverse: bfloat16 [512, 320, 320], P(('fine', 'tele')), may hold values from -0.08 to 0.45
- fine_links: int32 [512, 6], P(('fine', 'tele')), may hold values from -1 to 511, as said below
- fine_faces: int32 [512, 6], P(('fine', 'tele')), may hold values from 0 to 23
- coarse_inverse: bfloat16 [64, 320, 320], P(('fine', 'tele')), may hold values from -0.04 to 0.21
- coarse_links: int32 [64, 6], P(('fine', 'tele')), may hold values from -1 to 63, as said below
- coarse_faces: int32 [64, 6], P(('fine', 'tele')), may hold values from 0 to 23
- face_operators: bfloat16 [24, 80, 80], replicated, may hold values from -1.25 to 1.25
- agglomerate: int32 [512], P(('fine', 'tele')), may hold values from 0 to 63, as said below
Outputs:
- solution: float32 [512, 320], P(('fine', 'tele'))
Inputs may be any that keep to these rules, and one draw needn't show every extreme that they name: `fine_links`: any entry other than -1 is an element held by the same device as the element, or by the device just before or after it in the order of fine+tele, cyclically. `coarse_links`: coarse elements form blocks of 8 consecutive ones; any entry other than -1 lies in the element's own block or in the block just before or after it, cyclically. `agglomerate`: fine element i maps into block i // 64 of 8 consecutive coarse elements; every coarse element collects exactly 8 fine elements.
All inputs are finite; a program needn't handle non-finite values.
Results may differ from a plain program's by a relative error of at most 0.02.
Values may be sent and summed in bfloat16 or wider, within the bound.
A program may use at most 64 MiB of HBM per device.

v0:
```python
import jax
import jax.numpy as jnp
from jax import lax
from jax.sharding import PartitionSpec as P

FIELDS = 5
NODES = 4
SWEEPS = 3
CYCLES = 2


OPPOSITE = (1, 0, 3, 2, 5, 4)


def passed_along(block, axis, distance):
    devices = range(lax.axis_size(axis))
    route = [((i - distance) % len(devices), i) for i in devices]
    return lax.ppermute(block, axis, route)


def face_table():
    face_size = NODES * NODES
    column = jnp.arange(6 * FIELDS * face_size, dtype=jnp.int32)
    face_index = column // (FIELDS * face_size)
    within = column % (FIELDS * face_size)
    field_index = within // face_size
    first = within // NODES % NODES
    second = within % NODES
    far_node = NODES - 1
    side = jnp.where(face_index % 2 == 0, 0, far_node)
    node_a = jnp.where(face_index < 2, side, first)
    node_b = jnp.where(face_index < 2, first, jnp.where(face_index < 4, side, second))
    node_c = jnp.where(face_index < 4, second, side)
    target = ((field_index * NODES + node_a) * NODES + node_b) * NODES + node_c
    dof_index = jnp.arange(FIELDS * NODES * NODES * NODES, dtype=jnp.int32)
    return (dof_index[:, None] == target[None, :]).astype(jnp.float32)


def take_traces(field_state, table):
    row_count = field_state.shape[0]
    picked = jnp.dot(
        field_state, table, precision=lax.Precision.HIGHEST, preferred_element_type=jnp.float32
    )
    return picked.astype(jnp.bfloat16).reshape(row_count, 6, -1)


def lift_faces(coupled, table):
    return lax.dot_general(
        coupled,
        table,
        (((1,), (1,)), ((), ())),
        precision=lax.Precision.HIGHEST,
        preferred_element_type=jnp.float32,
    )


def neighbour_rows(preceding, own_traces, following, links, position, row_count, devices):
    trace_pool = jnp.concatenate([preceding, own_traces, following], axis=0).reshape(
        -1, own_traces.shape[2]
    )
    clamped = jnp.maximum(links, 0)
    relative = (clamped // row_count - position + 1) % devices
    opposite = jnp.array(OPPOSITE, jnp.int32)
    row_index = (relative * row_count + clamped % row_count) * 6 + opposite[None, :]
    face_rows = jnp.take(trace_pool, row_index.reshape(-1), axis=0).reshape(links.shape[0], 6, -1)
    return jnp.where((links >= 0)[:, :, None], face_rows, jnp.zeros_like(face_rows))


def face_apply(face_operators, face_rows, faces, table):
    flat_rows = face_rows.reshape(-1, face_rows.shape[2])
    face_kinds = faces.reshape(-1)
    products = jnp.einsum(
        "rk,qjk->rqj", flat_rows, face_operators, preferred_element_type=jnp.float32
    )
    picked = face_kinds[:, None] == jnp.arange(face_operators.shape[0], dtype=jnp.int32)[None, :]
    result = jnp.sum(jnp.where(picked[:, :, None], products, 0.0), axis=1)
    return lift_faces(result.reshape(face_rows.shape[0], -1), table)


def fine_coupling(field_state, face_operators, links, faces, position, devices, table):
    own_traces = take_traces(field_state, table)
    preceding = passed_along(own_traces, ("fine", "tele"), 1)
    following = passed_along(own_traces, ("fine", "tele"), -1)
    face_rows = neighbour_rows(
        preceding, own_traces, following, links, position, field_state.shape[0], devices
    )
    return face_apply(face_operators, face_rows, faces, table)


def coarse_coupling(column_traces, face_operators, links, faces, position, devices, table):
    preceding = passed_along(column_traces, "fine", 1)
    following = passed_along(column_traces, "fine", -1)
    face_rows = neighbour_rows(
        preceding, column_traces, following, links, position, column_traces.shape[0], devices
    )
    return face_apply(face_operators, face_rows, faces, table)


def apply_inverse(inverse, lowered):
    return jnp.einsum("nij,nj->ni", inverse, lowered, preferred_element_type=jnp.float32)


def shards(
    right_side,
    fine_inverse,
    fine_links,
    fine_faces,
    coarse_inverse,
    coarse_links,
    coarse_faces,
    face_operators,
    agglomerate,
):
    table = face_table()
    tele_size = lax.axis_size("tele")
    fine_position = lax.axis_index("fine") * tele_size + lax.axis_index("tele")
    fine_devices = lax.axis_size("fine") * tele_size
    column_position = lax.axis_index("fine")
    columns = lax.axis_size("fine")
    column_rows = coarse_inverse.shape[0] * tele_size
    local_target = agglomerate % column_rows
    member = (local_target[:, None] == jnp.arange(column_rows, dtype=jnp.int32)[None, :]).astype(
        jnp.float32
    )
    block_inverse = lax.all_gather(coarse_inverse, "tele", axis=0, tiled=True)
    index_lists = lax.all_gather(
        jnp.concatenate([coarse_links, coarse_faces], axis=1), "tele", axis=0, tiled=True
    )
    block_links = index_lists[:, :6]
    block_faces = index_lists[:, 6:]
    solution = jnp.zeros(right_side.shape, jnp.float32)
    for cycle_index in range(CYCLES):
        for sweep_index in range(SWEEPS):
            if cycle_index == 0 and sweep_index == 0:
                coupled = jnp.zeros(right_side.shape, jnp.float32)
            else:
                coupled = fine_coupling(
                    solution,
                    face_operators,
                    fine_links,
                    fine_faces,
                    fine_position,
                    fine_devices,
                    table,
                )
            lowered = (right_side - coupled).astype(jnp.bfloat16)
            solution = apply_inverse(fine_inverse, lowered)
        residual = lowered.astype(jnp.float32) - fine_coupling(
            solution, face_operators, fine_links, fine_faces, fine_position, fine_devices, table
        )
        partial_sum = jnp.dot(
            member.T, residual, precision=lax.Precision.HIGHEST, preferred_element_type=jnp.float32
        )
        restricted = lax.psum(partial_sum, "tele")
        coarse_state = apply_inverse(block_inverse, restricted.astype(jnp.bfloat16))
        for sweep_index in range(SWEEPS - 1):
            coupled_coarse = coarse_coupling(
                take_traces(coarse_state, table),
                face_operators,
                block_links,
                block_faces,
                column_position,
                columns,
                table,
            )
            coarse_state = apply_inverse(
                block_inverse, (restricted - coupled_coarse).astype(jnp.bfloat16)
            )
        solution = solution + jnp.take(coarse_state, local_target, axis=0)
    return solution


def solution(mesh):
    return jax.shard_map(
        shards,
        mesh=mesh,
        in_specs=(
            P(("fine", "tele"), None),
            P(("fine", "tele"), None, None),
            P(("fine", "tele"), None),
            P(("fine", "tele"), None),
            P(("fine", "tele"), None, None),
            P(("fine", "tele"), None),
            P(("fine", "tele"), None),
            P(),
            P(("fine", "tele")),
        ),
        out_specs=P(("fine", "tele"), None),
        check_vma=False,
    )
```

profile of v0, /device:TPU:0, one launch (start us, length us, event | category | flops | bytes accessed | tf_op | source)
XLA Modules:
  0.0 173.6 jit_solution(17787679589639048539)
XLA Ops:
  7.5 3.3 %fusion.76 = f32[16,1,320]{2,1,0:T(1,128)S(1)} fusion(bf16[16,320,320]{2,1,0:T(8,128)(2,1)} %param.27, bf16[16,320,1]{1,0,2:T(8,128)(2,1)S(1)} %convert_bitcast_fusion), kind=kOutput, calls=%fused_computation.136 | convolution fusion | flops 3276800 | bytes 3307520 | tf_op jit(solution)/shard_map/nij,nj->ni/dot_general | solution.py:100
  11.3 6.4 %collective-permute-start.1 = (bf16[16,6,80]{2,1,0:T(8,128)(2,1)S(1)}, bf16[16,6,80]{2,1,0:T(8,128)(2,1)S(1)}, u32[]{:S(2)}, u32[]{:S(2)}) collective-permute-start(bf16[16,6,80]{2,1,0:T(8,128)(2,1)S(1)} %reshape.333), channel_id=1, source_target_pairs={{1,0},{2,1},{3,2},{4,3},{5,4},{6,5},{7,6},{8,7},{9,8},{10,9},{11,1... | collective-permute-start | bytes 46088 | tf_op jit(solution)/shard_map/ppermute | solution.py:18
  17.8 5.1 %all-gather = s32[4,2,12]{2,1,0:T(2,128)S(1)} all-gather(s32[1,2,12]{2,1,0:T(2,128)S(1)} %add_bitcast_fusion), channel_id=1, replica_groups=mesh['fine'=8,'tele'=4] {'tele'}, dimensions={0}, use_global_device_ids=true | all-gather | bytes 480 | tf_op jit(solution)/shard_map/all_gather | solution.py:126
  26.3 3.5 %fusion.73 = f32[16,1,320]{2,1,0:T(1,128)S(1)} fusion(bf16[16,320,320]{2,1,0:T(8,128)(2,1)} %param.27, bf16[16,320,1]{1,0,2:T(8,128)(2,1)S(1)} %fusion.18), kind=kOutput, calls=%fused_computation.133 | convolution fusion | flops 3276800 | bytes 3307520 | tf_op jit(solution)/shard_map/nij,nj->ni/dot_general | solution.py:100
  30.3 3.5 %collective-permute-start.3 = (bf16[16,6,80]{2,1,0:T(8,128)(2,1)S(1)}, bf16[16,6,80]{2,1,0:T(8,128)(2,1)S(1)}, u32[]{:S(2)}, u32[]{:S(2)}) collective-permute-start(bf16[16,6,80]{2,1,0:T(8,128)(2,1)S(1)} %reshape.337), channel_id=1, source_target_pairs={{1,0},{2,1},{3,2},{4,3},{5,4},{6,5},{7,6},{8,7},{9,8},{10,9},{11,1... | collective-permute-start | bytes 46088 | tf_op jit(solution)/shard_map/ppermute | solution.py:18
  33.8 1.6 collective-permute-done.3
  35.4 5.4 %collective-permute-done.2 = bf16[16,6,80]{2,1,0:T(8,128)(2,1)S(1)} collective-permute-done((bf16[16,6,80]{2,1,0:T(8,128)(2,1)S(1)}, bf16[16,6,80]{2,1,0:T(8,128)(2,1)S(1)}, u32[]{:S(2)}, u32[]{:S(2)}) %collective-permute-start.2) | collective-permute-done | bytes 15392 | tf_op jit(solution)/shard_map/ppermute | solution.py:18
  42.6 3.3 %fusion.70 = f32[16,1,320]{2,1,0:T(1,128)S(1)} fusion(bf16[16,320,320]{2,1,0:T(8,128)(2,1)} %param.27, bf16[16,320,1]{1,0,2:T(8,128)(2,1)S(1)} %bitcast.138), kind=kOutput, calls=%fused_computation.130 | convolution fusion | flops 3276800 | bytes 3307520 | tf_op jit(solution)/shard_map/nij,nj->ni/dot_general | solution.py:100
  48.0 5.4 %collective-permute-done.4 = bf16[16,6,80]{2,1,0:T(8,128)(2,1)S(1)} collective-permute-done((bf16[16,6,80]{2,1,0:T(8,128)(2,1)S(1)}, bf16[16,6,80]{2,1,0:T(8,128)(2,1)S(1)}, u32[]{:S(2)}, u32[]{:S(2)}) %collective-permute-start.4) | collective-permute-done | bytes 15392 | tf_op jit(solution)/shard_map/ppermute | solution.py:18
  55.4 10.1 %psum.14 = f32[8,320]{1,0:T(8,128)S(1)} all-reduce(f32[8,320]{1,0:T(8,128)S(1)} %fusion.145), channel_id=1, replica_groups=mesh['fine'=8,'tele'=4] {'tele'}, use_global_device_ids=true, to_apply=%region_3.5 | all-reduce | flops 2560 | bytes 20480 | tf_op jit(solution)/shard_map/psum | solution.py:154
  65.5 2.3 %fusion.118 = f32[8,1,320]{2,1,0:T(1,128)S(1)} fusion(bf16[8,320,320]{2,1,0:T(8,128)(2,1)} %all-gather.3.cloned.1.call-done, bf16[8,320,1]{1,0,2:T(8,128)(2,1)S(1)} %convert_bitcast_fusion.2), kind=kOutput, calls=%fused_computation.187 | convolution fusion | flops 1638400 | bytes 1653760 | tf_op jit(solution)/shard_map/nij,nj->ni/dot_general | solution.py:100
  68.6 1.7 collective-permute-start.6
  70.4 1.8 %collective-permute-done.7 = bf16[8,6,80]{2,1,0:T(8,128)(2,1)S(1)} collective-permute-done((bf16[8,6,80]{2,1,0:T(8,128)(2,1)S(1)}, bf16[8,6,80]{2,1,0:T(8,128)(2,1)S(1)}, u32[]{:S(2)}, u32[]{:S(2)}) %collective-permute-start.7) | collective-permute-done | bytes 7712 | tf_op jit(solution)/shard_map/ppermute | solution.py:18
  72.2 2.8 %collective-permute-done.6 = bf16[8,6,80]{2,1,0:T(8,128)(2,1)S(1)} collective-permute-done((bf16[8,6,80]{2,1,0:T(8,128)(2,1)S(1)}, bf16[8,6,80]{2,1,0:T(8,128)(2,1)S(1)}, u32[]{:S(2)}, u32[]{:S(2)}) %collective-permute-start.6) | collective-permute-done | bytes 7712 | tf_op jit(solution)/shard_map/ppermute | solution.py:18
  76.6 2.3 %fusion.115 = f32[8,1,320]{2,1,0:T(1,128)S(1)} fusion(bf16[8,320,320]{2,1,0:T(8,128)(2,1)} %all-gather.3.cloned.1.call-done, bf16[8,320,1]{1,0,2:T(8,128)(2,1)S(1)} %fusion.26), kind=kOutput, calls=%fused_computation.184 | convolution fusion | flops 1638400 | bytes 1653760 | tf_op jit(solution)/shard_map/nij,nj->ni/dot_general | solution.py:100
  79.3 2.0 %collective-permute-start.8 = (bf16[8,6,80]{2,1,0:T(8,128)(2,1)S(1)}, bf16[8,6,80]{2,1,0:T(8,128)(2,1)S(1)}, u32[]{:S(2)}, u32[]{:S(2)}) collective-permute-start(bf16[8,6,80]{2,1,0:T(8,128)(2,1)S(1)} %reshape.349), channel_id=1, source_target_pairs={{28,0},{0,4},{4,8},{8,12},{12,16},{16,20},{20,24},{24,28},{29,1},{... | collective-permute-start | bytes 23048 | tf_op jit(solution)/shard_map/ppermute | solution.py:18
  81.3 1.7 collective-permute-done.9
  83.0 2.8 %collective-permute-done.8 = bf16[8,6,80]{2,1,0:T(8,128)(2,1)S(1)} collective-permute-done((bf16[8,6,80]{2,1,0:T(8,128)(2,1)S(1)}, bf16[8,6,80]{2,1,0:T(8,128)(2,1)S(1)}, u32[]{:S(2)}, u32[]{:S(2)}) %collective-permute-start.8) | collective-permute-done | bytes 7712 | tf_op jit(solution)/shard_map/ppermute | solution.py:18
  90.8 5.4 %collective-permute-done.10 = bf16[16,6,80]{2,1,0:T(8,128)(2,1)S(1)} collective-permute-done((bf16[16,6,80]{2,1,0:T(8,128)(2,1)S(1)}, bf16[16,6,80]{2,1,0:T(8,128)(2,1)S(1)}, u32[]{:S(2)}, u32[]{:S(2)}) %collective-permute-start.10) | collective-permute-done | bytes 15392 | tf_op jit(solution)/shard_map/ppermute | solution.py:18
  97.9 3.3 %fusion.68 = f32[16,1,320]{2,1,0:T(1,128)S(1)} fusion(bf16[16,320,320]{2,1,0:T(8,128)(2,1)} %param.27, bf16[16,320,1]{1,0,2:T(8,128)(2,1)S(1)} %fusion.17), kind=kOutput, calls=%fused_computation.128 | convolution fusion | flops 3276800 | bytes 3307520 | tf_op jit(solution)/shard_map/nij,nj->ni/dot_general | solution.py:100
  103.3 5.6 %collective-permute-done.12 = bf16[16,6,80]{2,1,0:T(8,128)(2,1)S(1)} collective-permute-done((bf16[16,6,80]{2,1,0:T(8,128)(2,1)S(1)}, bf16[16,6,80]{2,1,0:T(8,128)(2,1)S(1)}, u32[]{:S(2)}, u32[]{:S(2)}) %collective-permute-start.12) | collective-permute-done | bytes 15392 | tf_op jit(solution)/shard_map/ppermute | solution.py:18
  110.6 3.3 %fusion.65 = f32[16,1,320]{2,1,0:T(1,128)S(1)} fusion(bf16[16,320,320]{2,1,0:T(8,128)(2,1)} %param.27, bf16[16,320,1]{1,0,2:T(8,128)(2,1)S(1)} %fusion.16), kind=kOutput, calls=%fused_computation.125 | convolution fusion | flops 3276800 | bytes 3307520 | tf_op jit(solution)/shard_map/nij,nj->ni/dot_general | solution.py:100
  116.0 5.4 %collective-permute-done.14 = bf16[16,6,80]{2,1,0:T(8,128)(2,1)S(1)} collective-permute-done((bf16[16,6,80]{2,1,0:T(8,128)(2,1)S(1)}, bf16[16,6,80]{2,1,0:T(8,128)(2,1)S(1)}, u32[]{:S(2)}, u32[]{:S(2)}) %collective-permute-start.14) | collective-permute-done | bytes 15392 | tf_op jit(solution)/shard_map/ppermute | solution.py:18
  123.1 3.3 %fusion.62 = f32[16,1,320]{2,1,0:T(1,128)S(1)} fusion(bf16[16,320,320]{2,1,0:T(8,128)(2,1)} %param.27, bf16[16,320,1]{1,0,2:T(8,128)(2,1)S(1)} %bitcast.137), kind=kOutput, calls=%fused_computation.122 | convolution fusion | flops 3276800 | bytes 3307520 | tf_op jit(solution)/shard_map/nij,nj->ni/dot_general | solution.py:100
  128.5 5.4 %collective-permute-done.16 = bf16[16,6,80]{2,1,0:T(8,128)(2,1)S(1)} collective-permute-done((bf16[16,6,80]{2,1,0:T(8,128)(2,1)S(1)}, bf16[16,6,80]{2,1,0:T(8,128)(2,1)S(1)}, u32[]{:S(2)}, u32[]{:S(2)}) %collective-permute-start.16) | collective-permute-done | bytes 15392 | tf_op jit(solution)/shard_map/ppermute | solution.py:18
  135.9 10.1 %psum.15 = f32[8,320]{1,0:T(8,128)S(1)} all-reduce(f32[8,320]{1,0:T(8,128)S(1)} %fusion.144), channel_id=1, replica_groups=mesh['fine'=8,'tele'=4] {'tele'}, use_global_device_ids=true, to_apply=%region_10.14 | all-reduce | flops 2560 | bytes 20480 | tf_op jit(solution)/shard_map/psum | solution.py:154
  147.4 1.7 collective-permute-start.18
  149.1 1.9 %collective-permute-done.19 = bf16[8,6,80]{2,1,0:T(8,128)(2,1)S(1)} collective-permute-done((bf16[8,6,80]{2,1,0:T(8,128)(2,1)S(1)}, bf16[8,6,80]{2,1,0:T(8,128)(2,1)S(1)}, u32[]{:S(2)}, u32[]{:S(2)}) %collective-permute-start.19) | collective-permute-done | bytes 7712 | tf_op jit(solution)/shard_map/ppermute | solution.py:18
  151.0 2.9 %collective-permute-done.18 = bf16[8,6,80]{2,1,0:T(8,128)(2,1)S(1)} collective-permute-done((bf16[8,6,80]{2,1,0:T(8,128)(2,1)S(1)}, bf16[8,6,80]{2,1,0:T(8,128)(2,1)S(1)}, u32[]{:S(2)}, u32[]{:S(2)}) %collective-permute-start.18) | collective-permute-done | bytes 7712 | tf_op jit(solution)/shard_map/ppermute | solution.py:18
  156.6 2.0 %collective-permute-start.20 = (bf16[8,6,80]{2,1,0:T(8,128)(2,1)S(1)}, bf16[8,6,80]{2,1,0:T(8,128)(2,1)S(1)}, u32[]{:S(2)}, u32[]{:S(2)}) collective-permute-start(bf16[8,6,80]{2,1,0:T(8,128)(2,1)S(1)} %reshape.373), channel_id=1, source_target_pairs={{28,0},{0,4},{4,8},{8,12},{12,16},{16,20},{20,24},{24,28},{29,1},{... | collective-permute-start | bytes 23048 | tf_op jit(solution)/shard_map/ppermute | solution.py:18
  158.6 1.7 collective-permute-done.21
  160.3 2.8 %collective-permute-done.20 = bf16[8,6,80]{2,1,0:T(8,128)(2,1)S(1)} collective-permute-done((bf16[8,6,80]{2,1,0:T(8,128)(2,1)S(1)}, bf16[8,6,80]{2,1,0:T(8,128)(2,1)S(1)}, u32[]{:S(2)}, u32[]{:S(2)}) %collective-permute-start.20) | collective-permute-done | bytes 7712 | tf_op jit(solution)/shard_map/ppermute | solution.py:18
  (179 shorter events, 39.7 us)
Async XLA Ops:
  6.5 18.8 %copy-start = (bf16[24,80,80]{2,1,0:T(8,128)(2,1)S(1)}, bf16[24,80,80]{2,1,0:T(8,128)(2,1)}, u32[]{:S(2)}) copy-start(bf16[24,80,80]{2,1,0:T(8,128)(2,1)} %param.33) | copy-start | bytes 921604
  6.5 16.4 %copy-start.5 = (s32[6]{0:T(128)S(1)}, s32[6]{0:T(128)}, u32[]{:S(2)}) copy-start(s32[6]{0:T(128)} %constant.271.clone) | copy-start | bytes 76
  6.5 19.4 %copy-start.2 = (f32[16,320]{1,0:T(8,128)S(1)}, f32[16,320]{1,0:T(8,128)}, u32[]{:S(2)}) copy-start(f32[16,320]{1,0:T(8,128)} %param.26) | copy-start | bytes 61444
  6.5 11.2 %copy-start.3 = (s32[16,6]{0,1:T(8,128)S(1)}, s32[16,6]{0,1:T(8,128)}, u32[]{:S(2)}) copy-start(s32[16,6]{0,1:T(8,128)} %param.28) | copy-start | bytes 1156
  6.5 11.2 %copy-start.6 = (s32[2,6]{1,0:T(2,128)S(1)}, s32[2,6]{1,0:T(2,128)}, u32[]{:S(2)}) copy-start(s32[2,6]{1,0:T(2,128)} %param.32) | copy-start | bytes 148
  6.5 11.2 %copy-start.7 = (s32[2,6]{1,0:T(2,128)S(1)}, s32[2,6]{1,0:T(2,128)}, u32[]{:S(2)}) copy-start(s32[2,6]{1,0:T(2,128)} %param.31) | copy-start | bytes 148
  6.6 16.7 %copy-start.8 = (s32[16]{0:T(128)S(1)}, s32[16]{0:T(128)}, u32[]{:S(2)}) copy-start(s32[16]{0:T(128)} %param.34) | copy-start | bytes 196
  6.6 16.9 %copy-start.4 = (s32[16,6]{0,1:T(8,128)S(1)}, s32[16,6]{0,1:T(8,128)}, u32[]{:S(2)}) copy-start(s32[16,6]{0,1:T(8,128)} %param.29) | copy-start | bytes 1156
  6.6 58.9 %all-gather.3.cloned.1.call-start = ((), (), s32[]{:S(2)}) async-start(), calls=%async_computation | async-start | bytes 2457600 | tf_op jit(solution)/shard_map/all_gather | solution.py:125
  11.3 12.6 %collective-permute-start.1 = (bf16[16,6,80]{2,1,0:T(8,128)(2,1)S(1)}, bf16[16,6,80]{2,1,0:T(8,128)(2,1)S(1)}, u32[]{:S(2)}, u32[]{:S(2)}) collective-permute-start(bf16[16,6,80]{2,1,0:T(8,128)(2,1)S(1)} %reshape.333), channel_id=1, source_target_pairs={{1,0},{2,1},{3,2},{4,3},{5,4},{6,5},{7,6},{8,7},{9,8},{10,9},{11,1... | collective-permute-start | bytes 46088 | tf_op jit(solution)/shard_map/ppermute | solution.py:18
  17.7 6.9 %collective-permute-start = (bf16[16,6,80]{2,1,0:T(8,128)(2,1)S(1)}, bf16[16,6,80]{2,1,0:T(8,128)(2,1)S(1)}, u32[]{:S(2)}, u32[]{:S(2)}) collective-permute-start(bf16[16,6,80]{2,1,0:T(8,128)(2,1)S(1)} %reshape.333), channel_id=1, source_target_pairs={{31,0},{0,1},{1,2},{2,3},{3,4},{4,5},{5,6},{6,7},{7,8},{8,9},{9,10... | collective-permute-start | bytes 46088 | tf_op jit(solution)/shard_map/ppermute | solution.py:18
  30.3 5.1 %collective-permute-start.3 = (bf16[16,6,80]{2,1,0:T(8,128)(2,1)S(1)}, bf16[16,6,80]{2,1,0:T(8,128)(2,1)S(1)}, u32[]{:S(2)}, u32[]{:S(2)}) collective-permute-start(bf16[16,6,80]{2,1,0:T(8,128)(2,1)S(1)} %reshape.337), channel_id=1, source_target_pairs={{1,0},{2,1},{3,2},{4,3},{5,4},{6,5},{7,6},{8,7},{9,8},{10,9},{11,1... | collective-permute-start | bytes 46088 | tf_op jit(solution)/shard_map/ppermute | solution.py:18
  33.8 7.0 %collective-permute-start.2 = (bf16[16,6,80]{2,1,0:T(8,128)(2,1)S(1)}, bf16[16,6,80]{2,1,0:T(8,128)(2,1)S(1)}, u32[]{:S(2)}, u32[]{:S(2)}) collective-permute-start(bf16[16,6,80]{2,1,0:T(8,128)(2,1)S(1)} %reshape.337), channel_id=1, source_target_pairs={{31,0},{0,1},{1,2},{2,3},{3,4},{4,5},{5,6},{6,7},{7,8},{8,9},{9,10... | collective-permute-start | bytes 46088 | tf_op jit(solution)/shard_map/ppermute | solution.py:18
  46.3 1.7 collective-permute-start.5
  46.4 7.0 %collective-permute-start.4 = (bf16[16,6,80]{2,1,0:T(8,128)(2,1)S(1)}, bf16[16,6,80]{2,1,0:T(8,128)(2,1)S(1)}, u32[]{:S(2)}, u32[]{:S(2)}) collective-permute-start(bf16[16,6,80]{2,1,0:T(8,128)(2,1)S(1)} %reshape.341), channel_id=1, source_target_pairs={{31,0},{0,1},{1,2},{2,3},{3,4},{4,5},{5,6},{6,7},{7,8},{8,9},{9,10... | collective-permute-start | bytes 46088 | tf_op jit(solution)/shard_map/ppermute | solution.py:18
  65.5 22.0 %copy-start.1 = (bf16[8,320,320]{2,1,0:T(8,128)(2,1)S(1)}, bf16[8,320,320]{2,1,0:T(8,128)(2,1)}, u32[]{:S(2)}) copy-start(bf16[8,320,320]{2,1,0:T(8,128)(2,1)} %all-gather.3.cloned.1.call-done) | copy-start | bytes 4915204
  68.2 3.9 %collective-permute-start.7 = (bf16[8,6,80]{2,1,0:T(8,128)(2,1)S(1)}, bf16[8,6,80]{2,1,0:T(8,128)(2,1)S(1)}, u32[]{:S(2)}, u32[]{:S(2)}) collective-permute-start(bf16[8,6,80]{2,1,0:T(8,128)(2,1)S(1)} %reshape.345), channel_id=1, source_target_pairs={{4,0},{8,4},{12,8},{16,12},{20,16},{24,20},{28,24},{0,28},{5,1},{9... | collective-permute-start | bytes 23048 | tf_op jit(solution)/shard_map/ppermute | solution.py:18
  68.6 6.4 %collective-permute-start.6 = (bf16[8,6,80]{2,1,0:T(8,128)(2,1)S(1)}, bf16[8,6,80]{2,1,0:T(8,128)(2,1)S(1)}, u32[]{:S(2)}, u32[]{:S(2)}) collective-permute-start(bf16[8,6,80]{2,1,0:T(8,128)(2,1)S(1)} %reshape.345), channel_id=1, source_target_pairs={{28,0},{0,4},{4,8},{8,12},{12,16},{16,20},{20,24},{24,28},{29,1},{... | collective-permute-start | bytes 23048 | tf_op jit(solution)/shard_map/ppermute | solution.py:18
  79.3 3.8 %collective-permute-start.9 = (bf16[8,6,80]{2,1,0:T(8,128)(2,1)S(1)}, bf16[8,6,80]{2,1,0:T(8,128)(2,1)S(1)}, u32[]{:S(2)}, u32[]{:S(2)}) collective-permute-start(bf16[8,6,80]{2,1,0:T(8,128)(2,1)S(1)} %reshape.349), channel_id=1, source_target_pairs={{4,0},{8,4},{12,8},{16,12},{20,16},{24,20},{28,24},{0,28},{5,1},{9... | collective-permute-start | bytes 23048 | tf_op jit(solution)/shard_map/ppermute | solution.py:18
  79.3 6.5 %collective-permute-start.8 = (bf16[8,6,80]{2,1,0:T(8,128)(2,1)S(1)}, bf16[8,6,80]{2,1,0:T(8,128)(2,1)S(1)}, u32[]{:S(2)}, u32[]{:S(2)}) collective-permute-start(bf16[8,6,80]{2,1,0:T(8,128)(2,1)S(1)} %reshape.349), channel_id=1, source_target_pairs={{28,0},{0,4},{4,8},{8,12},{12,16},{16,20},{20,24},{24,28},{29,1},{... | collective-permute-start | bytes 23048 | tf_op jit(solution)/shard_map/ppermute | solution.py:18
  89.2 1.7 collective-permute-start.11
  89.2 7.0 %collective-permute-start.10 = (bf16[16,6,80]{2,1,0:T(8,128)(2,1)S(1)}, bf16[16,6,80]{2,1,0:T(8,128)(2,1)S(1)}, u32[]{:S(2)}, u32[]{:S(2)}) collective-permute-start(bf16[16,6,80]{2,1,0:T(8,128)(2,1)S(1)} %reshape.353), channel_id=1, source_target_pairs={{31,0},{0,1},{1,2},{2,3},{3,4},{4,5},{5,6},{6,7},{7,8},{8,9},{9,10... | collective-permute-start | bytes 46088 | tf_op jit(solution)/shard_map/ppermute | solution.py:18
  101.7 1.7 collective-permute-start.13
  101.7 7.2 %collective-permute-start.12 = (bf16[16,6,80]{2,1,0:T(8,128)(2,1)S(1)}, bf16[16,6,80]{2,1,0:T(8,128)(2,1)S(1)}, u32[]{:S(2)}, u32[]{:S(2)}) collective-permute-start(bf16[16,6,80]{2,1,0:T(8,128)(2,1)S(1)} %reshape.357), channel_id=1, source_target_pairs={{31,0},{0,1},{1,2},{2,3},{3,4},{4,5},{5,6},{6,7},{7,8},{8,9},{9,10... | collective-permute-start | bytes 46088 | tf_op jit(solution)/shard_map/ppermute | solution.py:18
  114.3 1.7 collective-permute-start.15
  114.4 7.0 %collective-permute-start.14 = (bf16[16,6,80]{2,1,0:T(8,128)(2,1)S(1)}, bf16[16,6,80]{2,1,0:T(8,128)(2,1)S(1)}, u32[]{:S(2)}, u32[]{:S(2)}) collective-permute-start(bf16[16,6,80]{2,1,0:T(8,128)(2,1)S(1)} %reshape.361), channel_id=1, source_target_pairs={{31,0},{0,1},{1,2},{2,3},{3,4},{4,5},{5,6},{6,7},{7,8},{8,9},{9,10... | collective-permute-start | bytes 46088 | tf_op jit(solution)/shard_map/ppermute | solution.py:18
  126.8 1.7 collective-permute-start.17
  126.9 7.0 %collective-permute-start.16 = (bf16[16,6,80]{2,1,0:T(8,128)(2,1)S(1)}, bf16[16,6,80]{2,1,0:T(8,128)(2,1)S(1)}, u32[]{:S(2)}, u32[]{:S(2)}) collective-permute-start(bf16[16,6,80]{2,1,0:T(8,128)(2,1)S(1)} %reshape.365), channel_id=1, source_target_pairs={{31,0},{0,1},{1,2},{2,3},{3,4},{4,5},{5,6},{6,7},{7,8},{8,9},{9,10... | collective-permute-start | bytes 46088 | tf_op jit(solution)/shard_map/ppermute | solution.py:18
  147.1 3.9 %collective-permute-start.19 = (bf16[8,6,80]{2,1,0:T(8,128)(2,1)S(1)}, bf16[8,6,80]{2,1,0:T(8,128)(2,1)S(1)}, u32[]{:S(2)}, u32[]{:S(2)}) collective-permute-start(bf16[8,6,80]{2,1,0:T(8,128)(2,1)S(1)} %reshape.369), channel_id=1, source_target_pairs={{4,0},{8,4},{12,8},{16,12},{20,16},{24,20},{28,24},{0,28},{5,1},{9... | collective-permute-start | bytes 23048 | tf_op jit(solution)/shard_map/ppermute | solution.py:18
  147.4 6.4 %collective-permute-start.18 = (bf16[8,6,80]{2,1,0:T(8,128)(2,1)S(1)}, bf16[8,6,80]{2,1,0:T(8,128)(2,1)S(1)}, u32[]{:S(2)}, u32[]{:S(2)}) collective-permute-start(bf16[8,6,80]{2,1,0:T(8,128)(2,1)S(1)} %reshape.369), channel_id=1, source_target_pairs={{28,0},{0,4},{4,8},{8,12},{12,16},{16,20},{20,24},{24,28},{29,1},{... | collective-permute-start | bytes 23048 | tf_op jit(solution)/shard_map/ppermute | solution.py:18
  156.6 3.8 %collective-permute-start.21 = (bf16[8,6,80]{2,1,0:T(8,128)(2,1)S(1)}, bf16[8,6,80]{2,1,0:T(8,128)(2,1)S(1)}, u32[]{:S(2)}, u32[]{:S(2)}) collective-permute-start(bf16[8,6,80]{2,1,0:T(8,128)(2,1)S(1)} %reshape.373), channel_id=1, source_target_pairs={{4,0},{8,4},{12,8},{16,12},{20,16},{24,20},{28,24},{0,28},{5,1},{9... | collective-permute-start | bytes 23048 | tf_op jit(solution)/shard_map/ppermute | solution.py:18
  156.6 6.5 %collective-permute-start.20 = (bf16[8,6,80]{2,1,0:T(8,128)(2,1)S(1)}, bf16[8,6,80]{2,1,0:T(8,128)(2,1)S(1)}, u32[]{:S(2)}, u32[]{:S(2)}) collective-permute-start(bf16[8,6,80]{2,1,0:T(8,128)(2,1)S(1)} %reshape.373), channel_id=1, source_target_pairs={{28,0},{0,4},{4,8},{8,12},{12,16},{16,20},{20,24},{24,28},{29,1},{... | collective-permute-start | bytes 23048 | tf_op jit(solution)/shard_map/ppermute | solution.py:18
Sparse Core Ops, SparseCore 0:
  17.8 23.7 all-gather.2
where the time goes:
time: 174 us
  waiting for transfers between devices  58.8 us (34%)
  matrix products  40.2 us (23%)
  blocking collectives  25.3 us (15%)
  starting transfers between devices  21 us (12%)
  between operations  14 us (8%)
  local copies, waits for them, and re-layouts  12.1 us (7%)
  other arithmetic  2.22 us (1%)
    ppermute x22, waiting for transfers between devices, passed_along(): return lax.ppermute(block, axis, route)  58.8 us
    dot_general x12, matrix products, apply_inverse(): jnp.einsum('nij,nj->ni', inverse, lowered, preferred_element_type=jnp.flo...  27.4 us
    ppermute x22, starting transfers between devices, passed_along(): return lax.ppermute(block, axis, route)  20.9 us
    psum x2, blocking collectives, shards(): restricted = lax.psum(partial_sum, 'tele')  20.3 us
    gather x11, local copies, waits for them, and re-layouts, neighbour_rows(): jnp.take(trace_pool, row_index.reshape(-1), axis=0)  7.2 us
    all_gather x1, blocking collectives, shards(): lax.all_gather(jnp.concatenate([coarse_links, coarse_faces], axis=1), 'te...  5.06 us
    dot_general x11, matrix products, face_apply(): jnp.einsum('rk,qjk->rqj', flat_rows, face_operators, preferred_element_ty...  4.72 us
    dot_general x11, matrix products, lift_faces(): lax.dot_general(coupled, table, (((1,), (1,)), ((), ())), precision=lax.P...  4 us
  transfers between devices with their start and end apart: 23, of which 21 were waited for; matrix products, arithmetic and copies ran while one was open for 8% of the time, Pallas kernels for 0%

commit v1 on v0

v1 whole, which is shorter than its diff:
```python
import functools

import jax
import jax.numpy as jnp
import numpy as np
from jax import lax
from jax.experimental import pallas as pl
from jax.experimental.pallas import tpu as pltpu
from jax.sharding import PartitionSpec as P

FIELDS = 5
NODES = 4
SWEEPS = 3
CYCLES = 2
FACES = 6
FACE_DOFS = FIELDS * NODES * NODES
DOFS = FIELDS * NODES**3
SLOT = 16
LANES = 128
MESH = pl.DeviceIdType.MESH
F32 = jnp.float32
BF16 = jnp.bfloat16


def face_targets():
    cube = np.arange(DOFS).reshape(FIELDS, NODES, NODES, NODES)
    far = NODES - 1
    slabs = (
        cube[:, 0], cube[:, far], cube[:, :, 0], cube[:, :, far], cube[..., 0], cube[..., far]
    )
    return [slab.reshape(-1) for slab in slabs]


def tables():
    targets = face_targets()
    trace = np.zeros((FACES * FACE_DOFS, DOFS), np.float32)
    lift = np.zeros((DOFS, FACES * FACE_DOFS), np.float32)
    for face in range(FACES):
        rows = face * FACE_DOFS + np.arange(FACE_DOFS)
        trace[rows, targets[face ^ 1]] = 1.0
        lift[targets[face], rows] = 1.0
    return jnp.asarray(trace, BF16), jnp.asarray(lift, BF16)


def dot(a, b):
    return jnp.dot(a, b, preferred_element_type=F32)


def dot_nt(a, b):
    return lax.dot_general(a, b, (((1,), (1,)), ((), ())), preferred_element_type=F32)


def split(value):
    high = value.astype(BF16)
    return high, (value - high.astype(F32)).astype(BF16)


def flip(value):
    rows, columns = value.shape
    pad_rows, pad_columns = -rows % LANES, -columns % LANES
    if pad_columns:
        value = jnp.concatenate([value, jnp.zeros((rows, pad_columns), F32)], axis=1)
    if pad_rows:
        value = jnp.concatenate([value, jnp.zeros((pad_rows, value.shape[1]), F32)], axis=0)
    return value.T[:columns, :rows]


def kernel(
    tele,
    fine_count,
    coarse_own,
    index_ref,
    slab_ref,
    right_ref,
    inverse_hbm,
    coarse_hbm,
    operators_ref,
    trace_ref,
    lift_ref,
    out_ref,
    inverse,
    coarse_inverse,
    slabs,
    operators,
    masked,
    fine_kinds,
    coarse_kinds,
    fine_pool,
    coarse_pool,
    partials,
    right,
    state,
    lowered,
    restricted,
    coarse_state,
    load_sem,
    own_sem,
    block_send,
    block_recv,
    slab_send,
    slab_recv,
    fine_send,
    fine_recv,
    coarse_send,
    coarse_recv,
    sum_send,
    sum_recv,
):
    types = operators_ref.shape[0]
    elements = right_ref.shape[0]
    coarse = coarse_own * tele
    fine = lax.axis_index("fine")
    place = lax.axis_index("tele")
    columns = fine_count

    def around(offset):
        position = lax.rem(fine * tele + place + offset + columns * tele, columns * tele)
        return (position // tele, lax.rem(position, tele))

    def column(offset):
        return (lax.rem(fine + offset + columns, columns), place)

    def peer(offset):
        return (fine, lax.rem(place + offset, tele))

    load = pltpu.make_async_copy(inverse_hbm, inverse, load_sem)
    load.start()
    own_rows = pl.ds(place * coarse_own, coarse_own)
    own_block = pltpu.make_async_copy(coarse_hbm, coarse_inverse.at[own_rows], own_sem)
    own_block.start()

    barrier = pltpu.get_barrier_semaphore()
    partners = [around(1), around(-1), column(1), column(-1)]
    partners += [peer(j) for j in range(1, tele)]
    for partner in partners:
        pl.semaphore_signal(barrier, inc=1, device_id=partner, device_id_type=MESH)

    operators[...] = jnp.zeros_like(operators)
    for kind in range(types):
        operators[:, kind * LANES : kind * LANES + FACE_DOFS] = operators_ref[kind]
    masked[...] = jnp.zeros_like(masked)
    right[...] = flip(right_ref[...])
    lowered[...] = right[...].astype(BF16)

    def gather_matrix(rows, width):
        wanted = lax.broadcasted_iota(jnp.int32, (LANES, LANES), 0)
        return (wanted == rows).astype(F32).T[:width, : 3 * SLOT].astype(BF16)

    def kind_masks(kinds, target, width):
        for kind in range(types):
            row = (kinds == kind).astype(F32)[:, :width]
            target[kind] = jnp.broadcast_to(row, (FACE_DOFS, width)).astype(BF16)

    fine_gather = gather_matrix(index_ref[0:1, :], FACES * elements)
    kind_masks(index_ref[1:2, :], fine_kinds, FACES * elements)
    member = (
        lax.broadcasted_iota(jnp.int32, (coarse, elements), 0) == index_ref[2:3, :elements]
    ).astype(F32).astype(BF16)

    pl.semaphore_wait(barrier, len(partners))

    setup = []
    for j in range(1, tele):
        setup.append(
            pltpu.make_async_remote_copy(
                src_ref=slab_ref,
                dst_ref=slabs.at[j],
                send_sem=slab_send.at[j],
                recv_sem=slab_recv.at[j],
                device_id=peer(j),
                device_id_type=MESH,
            )
        )
        setup.append(
            pltpu.make_async_remote_copy(
                src_ref=coarse_hbm,
                dst_ref=coarse_inverse.at[own_rows],
                send_sem=block_send.at[j],
                recv_sem=block_recv.at[j],
                device_id=peer(j),
                device_id_type=MESH,
            )
        )
    for copy in setup:
        copy.start()

    def apply_inverse(blocks, vectors, width):
        lane = lax.broadcasted_iota(jnp.int32, (DOFS, width), 1)
        total = jnp.zeros((DOFS, width), F32)
        for e in range(width):
            total = jnp.where(lane == e, dot(blocks[e], vectors), total)
        return total

    def exchange(pool, send, recv, step, partner, value):
        rows = flip(value)
        if rows.shape[0] < SLOT:
            rows = jnp.concatenate(
                [rows, jnp.zeros((SLOT - rows.shape[0], DOFS), F32)], axis=0
            )
        pool[step, SLOT : 2 * SLOT, :] = rows.astype(BF16)
        copies = [
            pltpu.make_async_remote_copy(
                src_ref=pool.at[step, pl.ds(SLOT, SLOT)],
                dst_ref=pool.at[step, pl.ds(landing * SLOT, SLOT)],
                send_sem=send.at[step, side],
                recv_sem=recv.at[step, side],
                device_id=partner(offset),
                device_id_type=MESH,
            )
            for side, (offset, landing) in enumerate(((1, 0), (-1, 2)))
        ]
        for copy in copies:
            copy.start()
        for copy in copies:
            copy.wait()
        return pool[step]

    def coupling(states, gather, kinds, width):
        picked = dot(gather, states).astype(BF16)
        traces = dot_nt(trace_ref[...], picked)
        lane_face = lax.broadcasted_iota(jnp.int32, (FACE_DOFS, FACES * width), 1) // width
        rows = traces[:FACE_DOFS]
        for face in range(1, FACES):
            rows = jnp.where(
                lane_face == face, traces[face * FACE_DOFS : (face + 1) * FACE_DOFS], rows
            )
        rows = rows.astype(BF16)
        span = FACES * width
        for kind in range(types):
            masked[kind * LANES : kind * LANES + FACE_DOFS, :span] = rows * kinds[kind]
        coupled = dot(operators[...], masked[:, :span]).astype(BF16)
        stacked = jnp.concatenate(
            [coupled[:, face * width : (face + 1) * width] for face in range(FACES)], axis=0
        )
        return dot(lift_ref[...], stacked)

    load.wait()
    state[...] = apply_inverse(inverse, lowered[...], elements)

    def fine_coupling(step):
        states = exchange(fine_pool, fine_send, fine_recv, step, around, state[...])
        return coupling(states, fine_gather, fine_kinds, elements)

    for cycle in range(CYCLES):
        base = cycle * (SWEEPS + 1)

        @pl.loop(1 if cycle == 0 else 0, SWEEPS)
        def sweep(s):
            low = (right[...] - fine_coupling(base + s)).astype(BF16)
            lowered[...] = low
            state[...] = apply_inverse(inverse, low, elements)

        residual = lowered[...].astype(F32) - fine_coupling(base + SWEEPS)
        high, low = split(residual)
        partials[cycle, 0] = dot_nt(member, high) + dot_nt(member, low)
        copies = [
            pltpu.make_async_remote_copy(
                src_ref=partials.at[cycle, 0],
                dst_ref=partials.at[cycle, j],
                send_sem=sum_send.at[cycle, j],
                recv_sem=sum_recv.at[cycle, j],
                device_id=peer(j),
                device_id_type=MESH,
            )
            for j in range(1, tele)
        ]
        for copy in copies:
            copy.start()
        if cycle == 0:
            own_block.wait()
            for copy in setup:
                copy.wait()
            slab = slab_ref[...]
            for j in range(1, tele):
                slab = slab + slabs[j]
            coarse_gather = gather_matrix(slab[0:1, :] - 1, FACES * coarse)
            kind_masks(slab[1:2, :], coarse_kinds, FACES * coarse)
        for copy in copies:
            copy.wait()
        total = partials[cycle, 0]
        for j in range(1, tele):
            total = total + partials[cycle, j]
        restricted[...] = flip(total)
        coarse_state[...] = apply_inverse(
            coarse_inverse, restricted[...].astype(BF16), coarse
        )

        @pl.loop(0, SWEEPS - 1)
        def coarse_sweep(s):
            states = exchange(
                coarse_pool,
                coarse_send,
                coarse_recv,
                cycle * (SWEEPS - 1) + s,
                column,
                coarse_state[...],
            )
            low = restricted[...] - coupling(states, coarse_gather, coarse_kinds, coarse)
            coarse_state[...] = apply_inverse(coarse_inverse, low.astype(BF16), coarse)

        high, low = split(coarse_state[...])
        state[...] = state[...] + dot(high, member) + dot(low, member)

    out_ref[...] = flip(state[...])


def row_of(values, width):
    flat = values.reshape(1, -1)
    return jnp.pad(flat, ((0, 0), (0, width - flat.shape[1])))


def pool_rows(links, position, row_count, devices):
    clamped = jnp.maximum(links, 0)
    relative = (clamped // row_count - position + 1) % devices
    return jnp.where(links >= 0, relative * SLOT + clamped % row_count, -1)


def shards(
    fine_size,
    tele,
    right_side,
    fine_inverse,
    fine_links,
    fine_faces,
    coarse_inverse,
    coarse_links,
    coarse_faces,
    face_operators,
    agglomerate,
):
    elements = right_side.shape[0]
    coarse_own = coarse_inverse.shape[0]
    coarse = coarse_own * tele
    types = face_operators.shape[0]
    fine = lax.axis_index("fine")
    place = lax.axis_index("tele")
    fine_rows = pool_rows(fine_links, fine * tele + place, elements, fine_size * tele)
    index = jnp.concatenate(
        [
            jnp.pad(
                row_of(fine_rows.T, FACES * elements),
                ((0, 0), (0, LANES - FACES * elements)),
                constant_values=-1,
            ),
            row_of(fine_faces.T, LANES),
            row_of(agglomerate % coarse, LANES),
            jnp.zeros((5, LANES), jnp.int32),
        ],
        axis=0,
    )
    coarse_rows = pool_rows(coarse_links, fine, coarse, fine_size) + 1

    def spread(values):
        own = (jnp.arange(coarse, dtype=jnp.int32) // coarse_own == place)[None, :]
        return row_of(jnp.where(own, jnp.tile(values.T, (1, tele)), 0), LANES)

    slab = jnp.concatenate(
        [spread(coarse_rows), spread(coarse_faces), jnp.zeros((6, LANES), jnp.int32)], axis=0
    )
    trace, lift = tables()
    rounds = CYCLES * (SWEEPS + 1)
    coarse_rounds = CYCLES * (SWEEPS - 1)
    vmem = pl.BlockSpec(memory_space=pltpu.VMEM)
    hbm = pl.BlockSpec(memory_space=pl.ANY)
    dma = pltpu.SemaphoreType.DMA
    return pl.pallas_call(
        functools.partial(kernel, tele, fine_size, coarse_own),
        out_shape=jax.ShapeDtypeStruct(right_side.shape, F32),
        in_specs=[vmem, vmem, vmem, hbm, hbm, vmem, vmem, vmem],
        out_specs=vmem,
        scratch_shapes=[
            pltpu.VMEM(fine_inverse.shape, BF16),
            pltpu.VMEM((coarse, DOFS, DOFS), BF16),
            pltpu.VMEM((tele, 8, LANES), jnp.int32),
            pltpu.VMEM((FACE_DOFS, types * LANES), BF16),
            pltpu.VMEM((types * LANES, FACES * elements), BF16),
            pltpu.VMEM((types, FACE_DOFS, FACES * elements), BF16),
            pltpu.VMEM((types, FACE_DOFS, FACES * coarse), BF16),
            pltpu.VMEM((rounds, 3 * SLOT, DOFS), BF16),
            pltpu.VMEM((coarse_rounds, 3 * SLOT, DOFS), BF16),
            pltpu.VMEM((CYCLES, tele, coarse, DOFS), F32),
            pltpu.VMEM((DOFS, elements), F32),
            pltpu.VMEM((DOFS, elements), F32),
            pltpu.VMEM((DOFS, elements), BF16),
            pltpu.VMEM((DOFS, coarse), F32),
            pltpu.VMEM((DOFS, coarse), F32),
            dma,
            dma,
            dma((tele,)),
            dma((tele,)),
            dma((tele,)),
            dma((tele,)),
            dma((rounds, 2)),
            dma((rounds, 2)),
            dma((coarse_rounds, 2)),
            dma((coarse_rounds, 2)),
            dma((CYCLES, tele)),
            dma((CYCLES, tele)),
        ],
        compiler_params=pltpu.CompilerParams(
            collective_id=0, has_side_effects=True, vmem_limit_bytes=40 * 2**20
        ),
        name="v_cycles",
    )(index, slab, right_side, fine_inverse, coarse_inverse, face_operators, trace, lift)


def solution(mesh):
    return jax.shard_map(
        functools.partial(shards, mesh.shape["fine"], mesh.shape["tele"]),
        mesh=mesh,
        in_specs=(
            P(("fine", "tele"), None),
            P(("fine", "tele"), None, None),
            P(("fine", "tele"), None),
            P(("fine", "tele"), None),
            P(("fine", "tele"), None, None),
            P(("fine", "tele"), None),
            P(("fine", "tele"), None),
            P(),
            P(("fine", "tele")),
        ),
        out_specs=P(("fine", "tele"), None),
        check_vma=False,
    )
```

time: 174 us -> 107 us (0.61)
  Pallas kernels: 0 us -> 94.9 us
  waiting for transfers between devices: 58.8 us -> 0 us
  matrix products: 40.2 us -> 0 us
  blocking collectives: 25.3 us -> 0 us
  starting transfers between devices: 21 us -> 0 us
  between operations: 14 us -> 0.04 us
  local copies, waits for them, and re-layouts: 12.1 us -> 9.64 us
    pallas_call x0 -> x1, Pallas kernels: none -> 94.9 us  [shards(): pl.pallas_call(functools.partial(kernel, tele, fine_size, coarse_own), ou...]
    ppermute x22 -> x0, waiting for transfers between devices: 58.8 us -> none  [passed_along(): return lax.ppermute(block, axis, route)]
    dot_general x47 -> x0, matrix products: 40.2 us -> none  [the longest x12 27.4 us: apply_inverse(): jnp.einsum('nij,nj->ni', inverse, lowered, preferred_element_type=jnp.flo...]
    ppermute x22 -> x0, starting transfers between devices: 20.9 us -> none  [passed_along(): return lax.ppermute(block, axis, route)]
    psum x2 -> x0, blocking collectives: 20.3 us -> none  [shards(): restricted = lax.psum(partial_sum, 'tele')]
    gather x13 -> x0, local copies, waits for them, and re-layouts: 8.38 us -> none  [the longest x11 7.2 us: neighbour_rows(): jnp.take(trace_pool, row_index.reshape(-1), axis=0)]
    unnamed x19 -> x13, local copies, waits for them, and re-layouts: 0.16 us -> 7.48 us
    all_gather x1 -> x0, blocking collectives: 5.06 us -> none  [shards(): lax.all_gather(jnp.concatenate([coarse_links, coarse_faces], axis=1), 'te...]
  transfers between devices with their start and end apart: 23 -> 0, of which waited for: 21 -> 0; matrix products, arithmetic and copies ran while one was open for 8% -> 0% of each run, Pallas kernels for 0% -> 0%
where the time goes in v1:
time: 107 us
  Pallas kernels  94.9 us (89%)
  local copies, waits for them, and re-layouts  9.64 us (9%)
  other arithmetic  2.16 us (2%)
    pallas_call x1, Pallas kernels, shards(): pl.pallas_call(functools.partial(kernel, tele, fine_size, coarse_own), ou...  94.9 us
    unnamed x13, local copies, waits for them, and re-layouts  7.48 us

profile of v1, /device:TPU:0, one launch (start us, length us, event | category | flops | bytes accessed | tf_op | source)
XLA Modules:
  0.0 106.7 jit_solution(16050280618936586353)
XLA Ops:
  0.0 0.8 reshape.76
  0.8 0.7 fusion.11
  1.5 0.7 fusion.17
  2.1 0.1 broadcast_in_dim.32
  2.2 0.1 pad.25.clone
  2.3 0.1 pad.29.clone
  2.4 0.1 copy.14
  2.5 0.7 fusion.6
  3.2 0.1 reshape.75
  3.3 0.8 copy.15
  4.0 0.1 tile.21
  4.2 0.1 tile.9
  4.3 0.1 fusion.7
  4.4 0.0 copy-start
  4.4 2.1 %copy-done = bf16[16,320,320]{2,1,0:T(8,128)(2,1)S(1)} copy-done((bf16[16,320,320]{2,1,0:T(8,128)(2,1)S(1)}, bf16[16,320,320]{2,1,0:T(8,128)(2,1)}, u32[]{:S(2)}) %copy-start) | copy-done | bytes 3276824
  6.5 0.0 copy-start.1
  6.5 1.0 copy-done.1
  7.5 0.0 copy-start.2
  7.5 1.0 copy-done.2
  8.5 0.0 copy-start.3
  8.5 1.0 copy-done.3
  9.5 0.0 copy-start.4
  9.5 1.0 copy-done.4
  10.5 0.0 copy-start.5
  10.5 0.7 copy-done.5
  11.2 94.9 %v_cycles.1 = f32[16,320]{1,0:T(8,128)S(1)} custom-call(s32[8,128]{1,0:T(8,128)S(1)} %get-tuple-element.8.index_ref, s32[8,128]{1,0:T(8,128)S(1)} %get-tuple-element.7.slab_ref, f32[16,320]{1,0:T(8,128)S(1)} %copy-done.5, bf16[16,320,320]{2,1,0:T(8,128)(2,1)S(1)} %copy-done, bf16[2,320,320]{2,1,0:T(8,128)(2,1)S(1)} %copy-done.1, ...), custom_call_target="tpu_custom_call" | custom-call | tf_op jit(solution)/shard_map/v_cycles/pallas_call | solution.py:366
  106.1 0.6 copy.17
  (7 shorter events, 0.0 us)
Async XLA Ops:
  4.4 2.1 %copy-start = (bf16[16,320,320]{2,1,0:T(8,128)(2,1)S(1)}, bf16[16,320,320]{2,1,0:T(8,128)(2,1)}, u32[]{:S(2)}) copy-start(bf16[16,320,320]{2,1,0:T(8,128)(2,1)} %inverse_hbm.1) | copy-start | bytes 9830404
  6.5 1.0 copy-start.1
  7.5 1.0 copy-start.2
  8.5 1.0 copy-start.3
  9.5 1.0 copy-start.4
  10.5 0.7 copy-start.5

commit v2 on v1

v2 whole, which is shorter than its diff:
```python
import functools

import jax
import jax.numpy as jnp
import numpy as np
from jax import lax
from jax.experimental import pallas as pl
from jax.experimental.pallas import tpu as pltpu
from jax.sharding import PartitionSpec as P

FIELDS = 5
NODES = 4
SWEEPS = 3
CYCLES = 2
FACES = 6
FACE_DOFS = FIELDS * NODES * NODES
DOFS = FIELDS * NODES**3
SLOT = 16
LANES = 128
MAIN = 256
TAIL = DOFS - MAIN
VMEM_BYTES = 60 * 2**20
MESH = pl.DeviceIdType.MESH
F32 = jnp.float32
BF16 = jnp.bfloat16


def face_targets():
    cube = np.arange(DOFS).reshape(FIELDS, NODES, NODES, NODES)
    far = NODES - 1
    slabs = (
        cube[:, 0], cube[:, far], cube[:, :, 0], cube[:, :, far], cube[..., 0], cube[..., far]
    )
    return [slab.reshape(-1) for slab in slabs]


def tables():
    targets = face_targets()
    trace = np.zeros((FACES * FACE_DOFS, DOFS), np.float32)
    lift = np.zeros((DOFS, FACES * FACE_DOFS), np.float32)
    for face in range(FACES):
        rows = face * FACE_DOFS + np.arange(FACE_DOFS)
        trace[rows, targets[face ^ 1]] = 1.0
        lift[targets[face], rows] = 1.0
    return jnp.asarray(trace, BF16), jnp.asarray(lift, BF16)


def dot(a, b):
    return jnp.dot(a, b, preferred_element_type=F32)


def dot_nt(a, b):
    return lax.dot_general(a, b, (((1,), (1,)), ((), ())), preferred_element_type=F32)


def split(value):
    high = value.astype(BF16)
    return high, (value - high.astype(F32)).astype(BF16)


def flip(value):
    rows, columns = value.shape
    pad_rows, pad_columns = -rows % LANES, -columns % LANES
    if pad_columns:
        value = jnp.concatenate([value, jnp.zeros((rows, pad_columns), F32)], axis=1)
    if pad_rows:
        value = jnp.concatenate([value, jnp.zeros((pad_rows, value.shape[1]), F32)], axis=0)
    return value.T[:columns, :rows]


def kernel(
    tele,
    fine_count,
    right_hbm,
    inverse_hbm,
    links_hbm,
    faces_hbm,
    coarse_hbm,
    coarse_links_ref,
    coarse_faces_ref,
    operators_hbm,
    agglomerate_ref,
    trace_hbm,
    lift_hbm,
    out_ref,
    raw,
    coarse_raw,
    inverse,
    coarse_inverse,
    right_in,
    links,
    faces,
    operators_in,
    trace,
    lift,
    slabs,
    operators,
    masked,
    fine_kinds,
    coarse_kinds,
    fine_gather,
    coarse_gather,
    fine_pool,
    coarse_pool,
    partials,
    right,
    state,
    lowered,
    coupled,
    restricted,
    coarse_state,
    coarse_coupled,
    load_sem,
    inverse_sem,
    own_sem,
    block_send,
    block_recv,
    slab_send,
    slab_recv,
    fine_send,
    fine_recv,
    coarse_send,
    coarse_recv,
    sum_send,
    sum_recv,
):
    types = operators_in.shape[0]
    elements = right_in.shape[0]
    coarse_own = coarse_links_ref.shape[0]
    coarse = coarse_own * tele
    fine = lax.axis_index("fine")
    place = lax.axis_index("tele")
    columns = fine_count
    position = fine * tele + place

    def around(offset):
        other = lax.rem(position + offset + columns * tele, columns * tele)
        return (other // tele, lax.rem(other, tele))

    def column(offset):
        return (lax.rem(fine + offset + columns, columns), place)

    def peer(offset):
        return (fine, lax.rem(place + offset, tele))

    pairs = (
        (right_hbm, right_in),
        (links_hbm, links),
        (faces_hbm, faces),
        (operators_hbm, operators_in),
        (trace_hbm, trace),
        (lift_hbm, lift),
    )
    loads = [
        pltpu.make_async_copy(source, target, load_sem.at[i])
        for i, (source, target) in enumerate(pairs)
    ]
    own_rows = pl.ds(place * coarse_own, coarse_own)
    own_block = pltpu.make_async_copy(coarse_hbm, coarse_raw.at[own_rows], own_sem)
    blocks = [
        pltpu.make_async_copy(inverse_hbm.at[e], raw.at[e], inverse_sem.at[e])
        for e in range(elements)
    ]
    for copy in loads + blocks + [own_block]:
        copy.start()

    barrier = pltpu.get_barrier_semaphore()
    partners = [around(1), around(-1), column(1), column(-1)]
    partners += [peer(j) for j in range(1, tele)]
    for partner in partners:
        pl.semaphore_signal(barrier, inc=1, device_id=partner, device_id_type=MESH)

    def gather_matrix(wanted, centre, count, owned):
        lane = lax.broadcasted_iota(jnp.int32, (1, 3 * SLOT), 1)
        target = jnp.full((1, 3 * SLOT), -2, jnp.int32)
        for slot in range(3):
            owner = lax.rem(centre + slot - 1 + count, count)
            inside = (lane >= slot * SLOT) & (lane < slot * SLOT + owned)
            target = jnp.where(inside, owner * owned + lane - slot * SLOT, target)
        return jnp.concatenate(
            [(wanted[:, face : face + 1] == target).astype(F32) for face in range(FACES)], axis=0
        ).astype(BF16)

    def kind_masks(kinds, target, width):
        turned = flip(kinds.astype(F32))
        row = jnp.concatenate([turned[face : face + 1] for face in range(FACES)], axis=1)
        for kind in range(types):
            chosen = (row == float(kind)).astype(F32)
            target[kind] = jnp.broadcast_to(chosen, (FACE_DOFS, FACES * width)).astype(BF16)

    coupled[...] = jnp.zeros_like(coupled)
    coarse_coupled[...] = jnp.zeros_like(coarse_coupled)
    slabs[place, 0, :coarse_own, :FACES] = coarse_links_ref[...]
    slabs[place, 1, :coarse_own, :FACES] = coarse_faces_ref[...]
    lane = lax.broadcasted_iota(jnp.int32, (coarse, elements), 1)
    target = jnp.zeros((coarse, elements), jnp.int32)
    for e in range(elements):
        target = jnp.where(lane == e, agglomerate_ref[e], target)
    row = lax.broadcasted_iota(jnp.int32, (coarse, elements), 0)
    member = (target == row + fine * coarse).astype(F32).astype(BF16)

    pl.semaphore_wait(barrier, len(partners))

    setup = []
    for j in range(1, tele):
        setup.append(
            pltpu.make_async_remote_copy(
                src_ref=slabs.at[place],
                dst_ref=slabs.at[place],
                send_sem=slab_send.at[j],
                recv_sem=slab_recv.at[j],
                device_id=peer(j),
                device_id_type=MESH,
            )
        )
        setup.append(
            pltpu.make_async_remote_copy(
                src_ref=coarse_hbm,
                dst_ref=coarse_raw.at[own_rows],
                send_sem=block_send.at[j],
                recv_sem=block_recv.at[j],
                device_id=peer(j),
                device_id_type=MESH,
            )
        )
    for copy in setup:
        copy.start()

    for copy in loads:
        copy.wait()
    right[...] = flip(right_in[...])
    operators[...] = jnp.concatenate([operators_in[kind] for kind in range(types)], axis=1)
    fine_gather[...] = gather_matrix(links[...], position, columns * tele, elements)
    kind_masks(faces[...], fine_kinds, elements)

    def pack(source, target, e):
        target[:, e * MAIN : (e + 1) * MAIN] = source[e, :, :MAIN]
        if e % 2:
            at = source.shape[0] * MAIN + (e - 1) * TAIL
            target[:, at : at + 2 * TAIL] = jnp.concatenate(
                [source[e - 1, :, MAIN:], source[e, :, MAIN:]], axis=1
            )

    def apply_inverse(packed, vectors, width):
        lane = lax.broadcasted_iota(jnp.int32, (1, width), 1)
        alone = [vectors * (lane == e).astype(F32).astype(BF16) for e in range(width)]
        spread = jnp.concatenate(
            [part[:MAIN] for part in alone] + [part[MAIN:] for part in alone], axis=0
        )
        return dot(packed[...], spread)

    def exchange(pool, send, recv, step, partner, value):
        rows = flip(value)
        if rows.shape[0] < SLOT:
            rows = jnp.concatenate(
                [rows, jnp.zeros((SLOT - rows.shape[0], DOFS), F32)], axis=0
            )
        pool[step, SLOT : 2 * SLOT, :] = rows.astype(BF16)
        copies = [
            pltpu.make_async_remote_copy(
                src_ref=pool.at[step, pl.ds(SLOT, SLOT)],
                dst_ref=pool.at[step, pl.ds(landing * SLOT, SLOT)],
                send_sem=send.at[step, side],
                recv_sem=recv.at[step, side],
                device_id=partner(offset),
                device_id_type=MESH,
            )
            for side, (offset, landing) in enumerate(((1, 0), (-1, 2)))
        ]
        for copy in copies:
            copy.start()
        for copy in copies:
            copy.wait()
        return pool[step]

    def coupling(states, gather, kinds, width):
        picked = dot(gather[...], states).astype(BF16)
        traces = dot_nt(trace[...], picked)
        span = FACES * width
        lane_face = lax.broadcasted_iota(jnp.int32, (FACE_DOFS, span), 1) // width
        rows = traces[:FACE_DOFS]
        for face in range(1, FACES):
            rows = jnp.where(
                lane_face == face, traces[face * FACE_DOFS : (face + 1) * FACE_DOFS], rows
            )
        rows = rows.astype(BF16)
        for kind in range(types):
            masked[kind * FACE_DOFS : (kind + 1) * FACE_DOFS, :span] = rows * kinds[kind]
        products = dot(operators[...], masked[:, :span]).astype(BF16)
        stacked = jnp.concatenate(
            [products[:, face * width : (face + 1) * width] for face in range(FACES)], axis=0
        )
        return dot(lift[...], stacked)

    for e in range(elements):
        blocks[e].wait()
        pack(raw, inverse, e)

    @pl.loop(0, CYCLES)
    def cycle_body(cycle):
        @pl.loop(0, SWEEPS + 1)
        def sweep_body(s):
            @pl.when(cycle + s > 0)
            def couple():
                states = exchange(
                    fine_pool, fine_send, fine_recv, cycle * (SWEEPS + 1) + s, around, state[...]
                )
                coupled[...] = coupling(states, fine_gather, fine_kinds, elements)

            @pl.when(s < SWEEPS)
            def relax():
                low = (right[...] - coupled[...]).astype(BF16)
                lowered[...] = low
                state[...] = apply_inverse(inverse, low, elements)

        high, low = split(lowered[...].astype(F32) - coupled[...])
        partials[cycle, 0] = dot_nt(member, high) + dot_nt(member, low)
        copies = [
            pltpu.make_async_remote_copy(
                src_ref=partials.at[cycle, 0],
                dst_ref=partials.at[cycle, j],
                send_sem=sum_send.at[cycle, j],
                recv_sem=sum_recv.at[cycle, j],
                device_id=peer(j),
                device_id_type=MESH,
            )
            for j in range(1, tele)
        ]
        for copy in copies:
            copy.start()

        @pl.when(cycle == 0)
        def finish_setup():
            own_block.wait()
            for copy in setup:
                copy.wait()
            wanted = jnp.concatenate(
                [slabs[t, 0, :coarse_own, :FACES] for t in range(tele)], axis=0
            )
            kinds = jnp.concatenate(
                [slabs[t, 1, :coarse_own, :FACES] for t in range(tele)], axis=0
            )
            coarse_gather[...] = gather_matrix(wanted, fine, columns, coarse)
            kind_masks(kinds, coarse_kinds, coarse)
            for e in range(coarse):
                pack(coarse_raw, coarse_inverse, e)

        for copy in copies:
            copy.wait()
        total = partials[cycle, 0]
        for j in range(1, tele):
            total = total + partials[cycle, j]
        restricted[...] = flip(total)

        @pl.loop(0, SWEEPS)
        def coarse_body(s):
            @pl.when(s > 0)
            def couple():
                states = exchange(
                    coarse_pool,
                    coarse_send,
                    coarse_recv,
                    cycle * (SWEEPS - 1) + s - 1,
                    column,
                    coarse_state[...],
                )
                coarse_coupled[...] = coupling(states, coarse_gather, coarse_kinds, coarse)

            low = restricted[...]
            low = jnp.where(s > 0, low - coarse_coupled[...], low).astype(BF16)
            coarse_state[...] = apply_inverse(coarse_inverse, low, coarse)

        high, low = split(coarse_state[...])
        state[...] = state[...] + dot(high, member) + dot(low, member)

    out_ref[...] = flip(state[...])


def shards(
    fine_size,
    tele,
    right_side,
    fine_inverse,
    fine_links,
    fine_faces,
    coarse_inverse,
    coarse_links,
    coarse_faces,
    face_operators,
    agglomerate,
):
    elements = right_side.shape[0]
    coarse = coarse_inverse.shape[0] * tele
    types = face_operators.shape[0]
    trace, lift = tables()
    rounds = CYCLES * (SWEEPS + 1)
    coarse_rounds = CYCLES * (SWEEPS - 1)
    vmem = pl.BlockSpec(memory_space=pltpu.VMEM)
    smem = pl.BlockSpec(memory_space=pltpu.SMEM)
    hbm = pl.BlockSpec(memory_space=pl.ANY)
    dma = pltpu.SemaphoreType.DMA
    return pl.pallas_call(
        functools.partial(kernel, tele, fine_size),
        out_shape=jax.ShapeDtypeStruct(right_side.shape, F32),
        in_specs=[hbm, hbm, hbm, hbm, hbm, vmem, vmem, hbm, smem, hbm, hbm],
        out_specs=vmem,
        scratch_shapes=[
            pltpu.VMEM(fine_inverse.shape, BF16),
            pltpu.VMEM((coarse, DOFS, DOFS), BF16),
            pltpu.VMEM((DOFS, elements * DOFS), BF16),
            pltpu.VMEM((DOFS, coarse * DOFS), BF16),
            pltpu.VMEM(right_side.shape, F32),
            pltpu.VMEM(fine_links.shape, jnp.int32),
            pltpu.VMEM(fine_faces.shape, jnp.int32),
            pltpu.VMEM(face_operators.shape, BF16),
            pltpu.VMEM(trace.shape, BF16),
            pltpu.VMEM(lift.shape, BF16),
            pltpu.VMEM((tele, 2, 8, LANES), jnp.int32),
            pltpu.VMEM((FACE_DOFS, types * FACE_DOFS), BF16),
            pltpu.VMEM((types * FACE_DOFS, FACES * elements), BF16),
            pltpu.VMEM((types, FACE_DOFS, FACES * elements), BF16),
            pltpu.VMEM((types, FACE_DOFS, FACES * coarse), BF16),
            pltpu.VMEM((FACES * elements, 3 * SLOT), BF16),
            pltpu.VMEM((FACES * coarse, 3 * SLOT), BF16),
            pltpu.VMEM((rounds, 3 * SLOT, DOFS), BF16),
            pltpu.VMEM((coarse_rounds, 3 * SLOT, DOFS), BF16),
            pltpu.VMEM((CYCLES, tele, coarse, DOFS), F32),
            pltpu.VMEM((DOFS, elements), F32),
            pltpu.VMEM((DOFS, elements), F32),
            pltpu.VMEM((DOFS, elements), BF16),
            pltpu.VMEM((DOFS, elements), F32),
            pltpu.VMEM((DOFS, coarse), F32),
            pltpu.VMEM((DOFS, coarse), F32),
            pltpu.VMEM((DOFS, coarse), F32),
            dma((6,)),
            dma((elements,)),
            dma,
            dma((tele,)),
            dma((tele,)),
            dma((tele,)),
            dma((tele,)),
            dma((rounds, 2)),
            dma((rounds, 2)),
            dma((coarse_rounds, 2)),
            dma((coarse_rounds, 2)),
            dma((CYCLES, tele)),
            dma((CYCLES, tele)),
        ],
        compiler_params=pltpu.CompilerParams(
            collective_id=0, has_side_effects=True, vmem_limit_bytes=VMEM_BYTES
        ),
        name="v_cycles",
    )(
        right_side,
        fine_inverse,
        fine_links,
        fine_faces,
        coarse_inverse,
        coarse_links,
        coarse_faces,
        face_operators,
        agglomerate,
        trace,
        lift,
    )


def solution(mesh):
    return jax.shard_map(
        functools.partial(shards, mesh.shape["fine"], mesh.shape["tele"]),
        mesh=mesh,
        in_specs=(
            P(("fine", "tele"), None),
            P(("fine", "tele"), None, None),
            P(("fine", "tele"), None),
            P(("fine", "tele"), None),
            P(("fine", "tele"), None, None),
            P(("fine", "tele"), None),
            P(("fine", "tele"), None),
            P(),
            P(("fine", "tele")),
        ),
        out_specs=P(("fine", "tele"), None),
        check_vma=False,
    )
```

time: 107 us -> 97.4 us (0.910)
  local copies, waits for them, and re-layouts: 9.64 us -> 4.06 us
  other arithmetic: 2.16 us -> 0 us
  Pallas kernels: 94.9 us -> 93.1 us
    unnamed x13 -> x3, local copies, waits for them, and re-layouts: 7.48 us -> 4.06 us
    pallas_call x1, Pallas kernels: 94.9 us -> 93.1 us  [shards(): pl.pallas_call(functools.partial(kernel, tele, fine_size), out_shape=jax....]
    transpose x2 -> x0, other arithmetic: 1.41 us -> none  [the longest x1 0.71 us: shards(): index = jnp.concatenate([jnp.pad(row_of(fine_rows.T, FACES * elements), (...]
where the time goes in v2:
time: 97.4 us; the launch traced here: 97.1 us
  Pallas kernels  93.1 us (96%)
  local copies, waits for them, and re-layouts  4.06 us (4%)
    pallas_call x1, Pallas kernels, shards(): pl.pallas_call(functools.partial(kernel, tele, fine_size), out_shape=jax....  93.1 us
    unnamed x3, local copies, waits for them, and re-layouts  4.06 us

profile of v2, /device:TPU:0, one launch (start us, length us, event | category | flops | bytes accessed | tf_op | source)
XLA Modules:
  0.0 97.1 jit_solution(4504198655288132072)
XLA Ops:
  0.0 1.4 %copy.12.links_hbm = s32[16,6]{1,0:T(8,128)} copy(s32[16,6]{0,1:T(8,128)} %param.13) | data formatting | bytes 768 | tf_op args[2]
  1.4 1.4 %copy.13.faces_hbm = s32[16,6]{1,0:T(8,128)} copy(s32[16,6]{0,1:T(8,128)} %param.14) | data formatting | bytes 768 | tf_op args[3]
  2.7 93.1 %v_cycles.1 = f32[16,320]{1,0:T(8,128)} custom-call(f32[16,320]{1,0:T(8,128)} %right_hbm.1, bf16[16,320,320]{2,1,0:T(8,128)(2,1)} %inverse_hbm.1, s32[16,6]{1,0:T(8,128)} %copy.12.links_hbm, s32[16,6]{1,0:T(8,128)} %copy.13.faces_hbm, bf16[2,320,320]{2,1,0:T(8,128)(2,1)} %coarse_hbm.1, s32[2,6]{1,0:T(2,128)} %coarse_links_ref.1, s32[2,6]{1,0:T(2,128)} %coarse_faces_ref.1, ...), custom_call_target="tpu_custom_call" | custom-call | tf_op jit(solution)/shard_map/v_cycles/pallas_call | solution.py:402
  95.8 1.3 %copy.15 = f32[16,320]{1,0:T(8,128)} copy(f32[16,320]{1,0:T(8,128)} %v_cycles.1) | data formatting | bytes 40960

commit v3 on v2

--- a/solution.py
+++ b/solution.py
@@ -12,6 +12,7 @@
 NODES = 4
 SWEEPS = 3
 CYCLES = 2
+CHUNKS = SWEEPS + 1
 FACES = 6
 FACE_DOFS = FIELDS * NODES * NODES
 DOFS = FIELDS * NODES**3
@@ -113,6 +114,8 @@
     load_sem,
     inverse_sem,
     own_sem,
+    near_send,
+    near_recv,
     block_send,
     block_recv,
     slab_send,
@@ -155,13 +158,12 @@
         pltpu.make_async_copy(source, target, load_sem.at[i])
         for i, (source, target) in enumerate(pairs)
     ]
-    own_rows = pl.ds(place * coarse_own, coarse_own)
-    own_block = pltpu.make_async_copy(coarse_hbm, coarse_raw.at[own_rows], own_sem)
+    own_block = pltpu.make_async_copy(coarse_hbm, coarse_raw, own_sem)
     blocks = [
         pltpu.make_async_copy(inverse_hbm.at[e], raw.at[e], inverse_sem.at[e])
         for e in range(elements)
     ]
-    for copy in loads + blocks + [own_block]:
+    for copy in [own_block] + loads + blocks:
         copy.start()
 
     barrier = pltpu.get_barrier_semaphore()
@@ -181,8 +183,7 @@
             [(wanted[:, face : face + 1] == target).astype(F32) for face in range(FACES)], axis=0
         ).astype(BF16)
 
-    def kind_masks(kinds, target, width):
-        turned = flip(kinds.astype(F32))
+    def kind_masks(turned, target, width):
         row = jnp.concatenate([turned[face : face + 1] for face in range(FACES)], axis=1)
         for kind in range(types):
             chosen = (row == float(kind)).astype(F32)
@@ -201,37 +202,62 @@
 
     pl.semaphore_wait(barrier, len(partners))
 
-    setup = []
-    for j in range(1, tele):
-        setup.append(
-            pltpu.make_async_remote_copy(
-                src_ref=slabs.at[place],
-                dst_ref=slabs.at[place],
-                send_sem=slab_send.at[j],
-                recv_sem=slab_recv.at[j],
-                device_id=peer(j),
-                device_id_type=MESH,
-            )
+    setup = [
+        pltpu.make_async_remote_copy(
+            src_ref=slabs.at[place],
+            dst_ref=slabs.at[place],
+            send_sem=slab_send.at[j],
+            recv_sem=slab_recv.at[j],
+            device_id=peer(j),
+            device_id_type=MESH,
         )
-        setup.append(
-            pltpu.make_async_remote_copy(
-                src_ref=coarse_hbm,
-                dst_ref=coarse_raw.at[own_rows],
-                send_sem=block_send.at[j],
-                recv_sem=block_recv.at[j],
-                device_id=peer(j),
-                device_id_type=MESH,
-            )
-        )
+        for j in range(1, tele)
+    ]
     for copy in setup:
         copy.start()
+
+    near = (fine, place + 1 - 2 * lax.rem(place, 2))
+    far_place = lax.rem(place + 2, tele)
+    far = (fine, far_place)
+    chunk_rows = DOFS // CHUNKS
+
+    def pack_own():
+        own_block.wait()
+        coarse_inverse[place, :, :MAIN] = coarse_raw[0, :, :MAIN]
+        coarse_inverse[place, :, MAIN : 2 * MAIN] = coarse_raw[1, :, :MAIN]
+        coarse_inverse[place, :, 2 * MAIN :] = jnp.concatenate(
+            [coarse_raw[0, :, MAIN:], coarse_raw[1, :, MAIN:]], axis=1
+        )
+
+    def chunk_copy(owner, chunk, leg, device):
+        part = coarse_inverse.at[owner, pl.ds(pl.multiple_of(chunk * chunk_rows, 16), chunk_rows)]
+        return pltpu.make_async_remote_copy(
+            src_ref=part,
+            dst_ref=part,
+            send_sem=block_send.at[leg, chunk],
+            recv_sem=block_recv.at[leg, chunk],
+            device_id=device,
+            device_id_type=MESH,
+        )
+
+    near_copy = pltpu.make_async_remote_copy(
+        src_ref=coarse_inverse.at[place],
+        dst_ref=coarse_inverse.at[place],
+        send_sem=near_send,
+        recv_sem=near_recv,
+        device_id=near,
+        device_id_type=MESH,
+    )
+    pack_own()
+    near_copy.start()
 
     for copy in loads:
         copy.wait()
     right[...] = flip(right_in[...])
     operators[...] = jnp.concatenate([operators_in[kind] for kind in range(types)], axis=1)
-    fine_gather[...] = gather_matrix(links[...], position, columns * tele, elements)
-    kind_masks(faces[...], fine_kinds, elements)
+    wanted = flip(links[...].astype(F32)).astype(jnp.int32)
+    fine_gather[...] = gather_matrix(wanted, position, columns * tele, elements)
+    kind_masks(faces[...].astype(F32), fine_kinds, elements)
 
     def pack(source, target, e):
         target[:, e * MAIN : (e + 1) * MAIN] = source[e, :, :MAIN]
@@ -244,10 +270,16 @@
     def apply_inverse(packed, vectors, width):
         lane = lax.broadcasted_iota(jnp.int32, (1, width), 1)
         alone = [vectors * (lane == e).astype(F32).astype(BF16) for e in range(width)]
-        spread = jnp.concatenate(
-            [part[:MAIN] for part in alone] + [part[MAIN:] for part in alone], axis=0
-        )
-        return dot(packed[...], spread)
+        group = width // len(packed)
+        total = None
+        for i, block in enumerate(packed):
+            own = alone[i * group : (i + 1) * group]
+            spread = jnp.concatenate(
+                [part[:MAIN] for part in own] + [part[MAIN:] for part in own], axis=0
+            )
+            product = dot(block, spread)
+            total = product if total is None else total + product
+        return total
 
     def exchange(pool, send, recv, step, partner, value):
         rows = flip(value)
@@ -296,6 +328,8 @@
         blocks[e].wait()
         pack(raw, inverse, e)
 
+    chunk_copy(place, 0, 0, far).start()
+
     @pl.loop(0, CYCLES)
     def cycle_body(cycle):
         @pl.loop(0, SWEEPS + 1)
@@ -305,13 +339,20 @@
                 states = exchange(
                     fine_pool, fine_send, fine_recv, cycle * (SWEEPS + 1) + s, around, state[...]
                 )
+
+                @pl.when(cycle == 0)
+                def pass_on():
+                    chunk_copy(place, s - 1, 0, far).wait_recv()
+                    chunk_copy(far_place, s - 1, 1, near).start()
+                    chunk_copy(place, s, 0, far).start()
+
                 coupled[...] = coupling(states, fine_gather, fine_kinds, elements)
 
             @pl.when(s < SWEEPS)
             def relax():
                 low = (right[...] - coupled[...]).astype(BF16)
                 lowered[...] = low
-                state[...] = apply_inverse(inverse, low, elements)
+                state[...] = apply_inverse([inverse[...]], low, elements)
 
         high, low = split(lowered[...].astype(F32) - coupled[...])
         partials[cycle, 0] = dot_nt(member, high) + dot_nt(member, low)
@@ -331,7 +372,9 @@
 
         @pl.when(cycle == 0)
         def finish_setup():
-            own_block.wait()
+            last = chunk_copy(place, CHUNKS - 1, 0, far)
+            last.wait_recv()
+            chunk_copy(far_place, CHUNKS - 1, 1, near).start()
             for copy in setup:
                 copy.wait()
             wanted = jnp.concatenate(
@@ -340,10 +383,13 @@
             kinds = jnp.concatenate(
                 [slabs[t, 1, :coarse_own, :FACES] for t in range(tele)], axis=0
             )
+            kinds = flip(kinds.astype(F32))
             coarse_gather[...] = gather_matrix(wanted, fine, columns, coarse)
             kind_masks(kinds, coarse_kinds, coarse)
-            for e in range(coarse):
-                pack(coarse_raw, coarse_inverse, e)
+            near_copy.wait()
+            for chunk in range(CHUNKS):
+                chunk_copy(place, chunk, 0, far).wait_send()
+                chunk_copy(far_place, chunk, 1, near).wait()
 
         for copy in copies:
             copy.wait()
@@ -368,7 +414,7 @@
 
             low = restricted[...]
             low = jnp.where(s > 0, low - coarse_coupled[...], low).astype(BF16)
-            coarse_state[...] = apply_inverse(coarse_inverse, low, coarse)
+            coarse_state[...] = apply_inverse([coarse_inverse[t] for t in range(tele)], low, coarse)
 
         high, low = split(coarse_state[...])
         state[...] = state[...] + dot(high, member) + dot(low, member)
@@ -390,7 +436,8 @@
     agglomerate,
 ):
     elements = right_side.shape[0]
-    coarse = coarse_inverse.shape[0] * tele
+    coarse_own = coarse_inverse.shape[0]
+    coarse = coarse_own * tele
     types = face_operators.shape[0]
     trace, lift = tables()
     rounds = CYCLES * (SWEEPS + 1)
@@ -406,12 +453,12 @@
         out_specs=vmem,
         scratch_shapes=[
             pltpu.VMEM(fine_inverse.shape, BF16),
-            pltpu.VMEM((coarse, DOFS, DOFS), BF16),
+            pltpu.VMEM(coarse_inverse.shape, BF16),
             pltpu.VMEM((DOFS, elements * DOFS), BF16),
-            pltpu.VMEM((DOFS, coarse * DOFS), BF16),
+            pltpu.VMEM((tele, DOFS, coarse_own * DOFS), BF16),
             pltpu.VMEM(right_side.shape, F32),
-            pltpu.VMEM(fine_links.shape, jnp.int32),
-            pltpu.VMEM(fine_faces.shape, jnp.int32),
+            pltpu.VMEM((FACES, elements), jnp.int32),
+            pltpu.VMEM((FACES, elements), jnp.int32),
             pltpu.VMEM(face_operators.shape, BF16),
             pltpu.VMEM(trace.shape, BF16),
             pltpu.VMEM(lift.shape, BF16),
@@ -435,8 +482,10 @@
             dma((6,)),
             dma((elements,)),
             dma,
-            dma((tele,)),
-            dma((tele,)),
+            dma,
+            dma,
+            dma((2, CHUNKS)),
+            dma((2, CHUNKS)),
             dma((tele,)),
             dma((tele,)),
             dma((rounds, 2)),
@@ -453,8 +502,8 @@
     )(
         right_side,
         fine_inverse,
-        fine_links,
-        fine_faces,
+        fine_links.T,
+        fine_faces.T,
         coarse_inverse,
         coarse_links,
         coarse_faces,

time: 97.4 us -> 81.6 us (0.84)
  Pallas kernels: 93.1 us -> 80.1 us
  local copies, waits for them, and re-layouts: 4.06 us -> 1.35 us
    pallas_call x1, Pallas kernels: 93.1 us -> 80.1 us  [shards(): pl.pallas_call(functools.partial(kernel, tele, fine_size), out_shape=jax....]
    unnamed x3 -> x1, local copies, waits for them, and re-layouts: 4.06 us -> 1.35 us
where the time goes in v3:
time: 81.6 us; the launch traced here: 81.5 us
  Pallas kernels  80.1 us (98%)
  local copies, waits for them, and re-layouts  1.35 us (2%)
    pallas_call x1, Pallas kernels, shards(): pl.pallas_call(functools.partial(kernel, tele, fine_size), out_shape=jax....  80.1 us

profile of v3, /device:TPU:0, one launch (start us, length us, event | category | flops | bytes accessed | tf_op | source)
XLA Modules:
  0.0 81.5 jit_solution(14261693751667983495)
XLA Ops:
  0.0 80.1 %v_cycles.1 = f32[16,320]{1,0:T(8,128)} custom-call(f32[16,320]{1,0:T(8,128)} %right_hbm.1, bf16[16,320,320]{2,1,0:T(8,128)(2,1)} %inverse_hbm.1, s32[6,16]{1,0:T(8,128)} %bitcast.2, s32[6,16]{1,0:T(8,128)} %bitcast.3, bf16[2,320,320]{2,1,0:T(8,128)(2,1)} %coarse_hbm.1, s32[2,6]{1,0:T(2,128)} %coarse_links_ref.1, s32[2,6]{1,0:T(2,128)} %coarse_faces_ref.1, ...), custom_call_target="tpu_custom_call" | custom-call | tf_op jit(solution)/shard_map/v_cycles/pallas_call | solution.py:449
  80.1 1.3 %copy.13 = f32[16,320]{1,0:T(8,128)} copy(f32[16,320]{1,0:T(8,128)} %v_cycles.1) | data formatting | bytes 40960

commit v4 on v3

--- a/solution.py
+++ b/solution.py
@@ -77,10 +77,10 @@
     links_hbm,
     faces_hbm,
     coarse_hbm,
-    coarse_links_ref,
-    coarse_faces_ref,
+    coarse_links_hbm,
+    coarse_faces_hbm,
     operators_hbm,
-    agglomerate_ref,
+    agglomerate_hbm,
     trace_hbm,
     lift_hbm,
     out_ref,
@@ -94,6 +94,10 @@
     operators_in,
     trace,
     lift,
+    coarse_links,
+    coarse_faces,
+    targets,
+    member,
     slabs,
     operators,
     masked,
@@ -129,7 +133,7 @@
 ):
     types = operators_in.shape[0]
     elements = right_in.shape[0]
-    coarse_own = coarse_links_ref.shape[0]
+    coarse_own = coarse_links.shape[0]
     coarse = coarse_own * tele
     fine = lax.axis_index("fine")
     place = lax.axis_index("tele")
@@ -153,6 +157,9 @@
         (operators_hbm, operators_in),
         (trace_hbm, trace),
         (lift_hbm, lift),
+        (coarse_links_hbm, coarse_links),
+        (coarse_faces_hbm, coarse_faces),
+        (agglomerate_hbm, targets),
     )
     loads = [
         pltpu.make_async_copy(source, target, load_sem.at[i])
@@ -163,7 +170,7 @@
         pltpu.make_async_copy(inverse_hbm.at[e], raw.at[e], inverse_sem.at[e])
         for e in range(elements)
     ]
-    for copy in [own_block] + loads + blocks:
+    for copy in loads[:1] + blocks + [own_block] + loads[1:]:
         copy.start()
 
     barrier = pltpu.get_barrier_semaphore()
@@ -191,14 +198,6 @@
 
     coupled[...] = jnp.zeros_like(coupled)
     coarse_coupled[...] = jnp.zeros_like(coarse_coupled)
-    slabs[place, 0, :coarse_own, :FACES] = coarse_links_ref[...]
-    slabs[place, 1, :coarse_own, :FACES] = coarse_faces_ref[...]
-    lane = lax.broadcasted_iota(jnp.int32, (coarse, elements), 1)
-    target = jnp.zeros((coarse, elements), jnp.int32)
-    for e in range(elements):
-        target = jnp.where(lane == e, agglomerate_ref[e], target)
-    row = lax.broadcasted_iota(jnp.int32, (coarse, elements), 0)
-    member = (target == row + fine * coarse).astype(F32).astype(BF16)
 
     pl.semaphore_wait(barrier, len(partners))
 
@@ -213,8 +212,6 @@
         )
         for j in range(1, tele)
     ]
-    for copy in setup:
-        copy.start()
 
     near = (fine, place + 1 - 2 * lax.rem(place, 2))
     far_place = lax.rem(place + 2, tele)
@@ -248,16 +245,23 @@
         device_id=near,
         device_id_type=MESH,
     )
-    pack_own()
-    near_copy.start()
-
-    for copy in loads:
-        copy.wait()
-    right[...] = flip(right_in[...])
-    operators[...] = jnp.concatenate([operators_in[kind] for kind in range(types)], axis=1)
-    wanted = flip(links[...].astype(F32)).astype(jnp.int32)
-    fine_gather[...] = gather_matrix(wanted, position, columns * tele, elements)
-    kind_masks(faces[...].astype(F32), fine_kinds, elements)
+    def fine_tables():
+        for copy in loads[1:]:
+            copy.wait()
+        operators[...] = jnp.concatenate([operators_in[kind] for kind in range(types)], axis=1)
+        wanted = flip(links[...].astype(F32)).astype(jnp.int32)
+        fine_gather[...] = gather_matrix(wanted, position, columns * tele, elements)
+        kind_masks(faces[...].astype(F32), fine_kinds, elements)
+        slabs[place, 0, :coarse_own, :FACES] = coarse_links[...]
+        slabs[place, 1, :coarse_own, :FACES] = coarse_faces[...]
+        for copy in setup:
+            copy.start()
+        lane = lax.broadcasted_iota(jnp.int32, (coarse, elements), 1)
+        target = jnp.zeros((coarse, elements), jnp.int32)
+        for e in range(elements):
+            target = jnp.where(lane == e, targets[e], target)
+        row = lax.broadcasted_iota(jnp.int32, (coarse, elements), 0)
+        member[...] = (target == row + fine * coarse).astype(F32).astype(BF16)
 
     def pack(source, target, e):
         target[:, e * MAIN : (e + 1) * MAIN] = source[e, :, :MAIN]
@@ -281,7 +285,7 @@
             total = product if total is None else total + product
         return total
 
-    def exchange(pool, send, recv, step, partner, value):
+    def exchange(pool, send, recv, step, partner, value, meanwhile=lambda: None):
         rows = flip(value)
         if rows.shape[0] < SLOT:
             rows = jnp.concatenate(
@@ -301,6 +305,7 @@
         ]
         for copy in copies:
             copy.start()
+        meanwhile()
         for copy in copies:
             copy.wait()
         return pool[step]
@@ -309,11 +314,11 @@
         picked = dot(gather[...], states).astype(BF16)
         traces = dot_nt(trace[...], picked)
         span = FACES * width
-        lane_face = lax.broadcasted_iota(jnp.int32, (FACE_DOFS, span), 1) // width
+        lane = lax.broadcasted_iota(jnp.int32, (FACE_DOFS, span), 1)
         rows = traces[:FACE_DOFS]
         for face in range(1, FACES):
             rows = jnp.where(
-                lane_face == face, traces[face * FACE_DOFS : (face + 1) * FACE_DOFS], rows
+                lane >= face * width, traces[face * FACE_DOFS : (face + 1) * FACE_DOFS], rows
             )
         rows = rows.astype(BF16)
         for kind in range(types):
@@ -324,10 +329,14 @@
         )
         return dot(lift[...], stacked)
 
+    loads[0].wait()
+    right[...] = flip(right_in[...])
     for e in range(elements):
         blocks[e].wait()
         pack(raw, inverse, e)
 
+    pack_own()
+    near_copy.start()
     chunk_copy(place, 0, 0, far).start()
 
     @pl.loop(0, CYCLES)
@@ -336,8 +345,17 @@
         def sweep_body(s):
             @pl.when(cycle + s > 0)
             def couple():
+                def meanwhile():
+                    pl.when(cycle * (SWEEPS + 1) + s == 1)(fine_tables)
+
                 states = exchange(
-                    fine_pool, fine_send, fine_recv, cycle * (SWEEPS + 1) + s, around, state[...]
+                    fine_pool,
+                    fine_send,
+                    fine_recv,
+                    cycle * (SWEEPS + 1) + s,
+                    around,
+                    state[...],
+                    meanwhile,
                 )
 
                 @pl.when(cycle == 0)
@@ -355,7 +373,7 @@
                 state[...] = apply_inverse([inverse[...]], low, elements)
 
         high, low = split(lowered[...].astype(F32) - coupled[...])
-        partials[cycle, 0] = dot_nt(member, high) + dot_nt(member, low)
+        partials[cycle, 0] = dot_nt(member[...], high) + dot_nt(member[...], low)
         copies = [
             pltpu.make_async_remote_copy(
                 src_ref=partials.at[cycle, 0],
@@ -417,7 +435,7 @@
             coarse_state[...] = apply_inverse([coarse_inverse[t] for t in range(tele)], low, coarse)
 
         high, low = split(coarse_state[...])
-        state[...] = state[...] + dot(high, member) + dot(low, member)
+        state[...] = state[...] + dot(high, member[...]) + dot(low, member[...])
 
     out_ref[...] = flip(state[...])
 
@@ -443,13 +461,12 @@
     rounds = CYCLES * (SWEEPS + 1)
     coarse_rounds = CYCLES * (SWEEPS - 1)
     vmem = pl.BlockSpec(memory_space=pltpu.VMEM)
-    smem = pl.BlockSpec(memory_space=pltpu.SMEM)
-    hbm = pl.BlockSpec(memory_space=pl.ANY)
+    hbm = pl.BlockSpec(memory_space=pltpu.HBM)
     dma = pltpu.SemaphoreType.DMA
     return pl.pallas_call(
         functools.partial(kernel, tele, fine_size),
         out_shape=jax.ShapeDtypeStruct(right_side.shape, F32),
-        in_specs=[hbm, hbm, hbm, hbm, hbm, vmem, vmem, hbm, smem, hbm, hbm],
+        in_specs=[hbm] * 11,
         out_specs=vmem,
         scratch_shapes=[
             pltpu.VMEM(fine_inverse.shape, BF16),
@@ -462,6 +479,10 @@
             pltpu.VMEM(face_operators.shape, BF16),
             pltpu.VMEM(trace.shape, BF16),
             pltpu.VMEM(lift.shape, BF16),
+            pltpu.VMEM(coarse_links.shape, jnp.int32),
+            pltpu.VMEM(coarse_faces.shape, jnp.int32),
+            pltpu.SMEM(agglomerate.shape, jnp.int32),
+            pltpu.VMEM((coarse, elements), BF16),
             pltpu.VMEM((tele, 2, 8, LANES), jnp.int32),
             pltpu.VMEM((FACE_DOFS, types * FACE_DOFS), BF16),
             pltpu.VMEM((types * FACE_DOFS, FACES * elements), BF16),
@@ -479,7 +500,7 @@
             pltpu.VMEM((DOFS, coarse), F32),
             pltpu.VMEM((DOFS, coarse), F32),
             pltpu.VMEM((DOFS, coarse), F32),
-            dma((6,)),
+            dma((9,)),
             dma((elements,)),
             dma,
             dma,

time: 81.6 us -> 80.3 us (0.984)
  Pallas kernels: 80.1 us -> 78.8 us
    pallas_call x1, Pallas kernels: 80.1 us -> 78.8 us  [shards(): pl.pallas_call(functools.partial(kernel, tele, fine_size), out_shape=jax....]
where the time goes in v4:
time: 80.3 us; the launch traced here: 80.2 us
  Pallas kernels  78.8 us (98%)
  local copies, waits for them, and re-layouts  1.35 us (2%)
    pallas_call x1, Pallas kernels, shards(): pl.pallas_call(functools.partial(kernel, tele, fine_size), out_shape=jax....  78.8 us

profile of v4, /device:TPU:0, one launch (start us, length us, event | category | flops | bytes accessed | tf_op | source)
XLA Modules:
  0.0 80.2 jit_solution(15037354503553458556)
XLA Ops:
  0.0 78.8 %v_cycles.1 = f32[16,320]{1,0:T(8,128)} custom-call(f32[16,320]{1,0:T(8,128)} %right_hbm.1, bf16[16,320,320]{2,1,0:T(8,128)(2,1)} %inverse_hbm.1, s32[6,16]{1,0:T(8,128)} %bitcast.2, s32[6,16]{1,0:T(8,128)} %bitcast.3, bf16[2,320,320]{2,1,0:T(8,128)(2,1)} %coarse_hbm.1, s32[2,6]{1,0:T(2,128)} %coarse_links_hbm.1, s32[2,6]{1,0:T(2,128)} %coarse_faces_hbm.1, ...), custom_call_target="tpu_custom_call" | custom-call | tf_op jit(solution)/shard_map/v_cycles/pallas_call | solution.py:466
  78.8 1.3 %copy.13 = f32[16,320]{1,0:T(8,128)} copy(f32[16,320]{1,0:T(8,128)} %v_cycles.1) | data formatting | bytes 40960

commit v5 on v4

--- a/solution.py
+++ b/solution.py
@@ -35,15 +35,11 @@
     return [slab.reshape(-1) for slab in slabs]
 
 
-def tables():
-    targets = face_targets()
-    trace = np.zeros((FACES * FACE_DOFS, DOFS), np.float32)
-    lift = np.zeros((DOFS, FACES * FACE_DOFS), np.float32)
-    for face in range(FACES):
-        rows = face * FACE_DOFS + np.arange(FACE_DOFS)
-        trace[rows, targets[face ^ 1]] = 1.0
-        lift[targets[face], rows] = 1.0
-    return jnp.asarray(trace, BF16), jnp.asarray(lift, BF16)
+def face_nodes():
+    table = np.zeros((DOFS, FACES * LANES), np.float32)
+    for face, nodes in enumerate(face_targets()):
+        table[nodes, face * LANES + np.arange(FACE_DOFS)] = 1.0
+    return jnp.asarray(table, BF16)
 
 
 def dot(a, b):
@@ -81,8 +77,7 @@
     coarse_faces_hbm,
     operators_hbm,
     agglomerate_hbm,
-    trace_hbm,
-    lift_hbm,
+    nodes_hbm,
     out_ref,
     raw,
     coarse_raw,
@@ -92,15 +87,13 @@
     links,
     faces,
     operators_in,
-    trace,
-    lift,
+    nodes,
     coarse_links,
     coarse_faces,
     targets,
     member,
     slabs,
     operators,
-    masked,
     fine_kinds,
     coarse_kinds,
     fine_gather,
@@ -152,11 +145,10 @@
 
     pairs = (
         (right_hbm, right_in),
+        (nodes_hbm, nodes),
         (links_hbm, links),
         (faces_hbm, faces),
         (operators_hbm, operators_in),
-        (trace_hbm, trace),
-        (lift_hbm, lift),
         (coarse_links_hbm, coarse_links),
         (coarse_faces_hbm, coarse_faces),
         (agglomerate_hbm, targets),
@@ -186,15 +178,13 @@
             owner = lax.rem(centre + slot - 1 + count, count)
             inside = (lane >= slot * SLOT) & (lane < slot * SLOT + owned)
             target = jnp.where(inside, owner * owned + lane - slot * SLOT, target)
-        return jnp.concatenate(
-            [(wanted[:, face : face + 1] == target).astype(F32) for face in range(FACES)], axis=0
-        ).astype(BF16)
-
-    def kind_masks(turned, target, width):
-        row = jnp.concatenate([turned[face : face + 1] for face in range(FACES)], axis=1)
+        return [(wanted[:, face : face + 1] == target).astype(F32) for face in range(FACES)]
+
+    def kind_masks(kinds, target):
+        column = jnp.concatenate([kinds[:, face : face + 1] for face in range(FACES)], axis=0)
         for kind in range(types):
-            chosen = (row == float(kind)).astype(F32)
-            target[kind] = jnp.broadcast_to(chosen, (FACE_DOFS, FACES * width)).astype(BF16)
+            chosen = (column == kind).astype(F32)
+            target[kind] = jnp.broadcast_to(chosen, target.shape[1:]).astype(BF16)
 
     coupled[...] = jnp.zeros_like(coupled)
     coarse_coupled[...] = jnp.zeros_like(coarse_coupled)
@@ -246,12 +236,18 @@
         device_id_type=MESH,
     )
     def fine_tables():
-        for copy in loads[1:]:
+        for copy in loads[2:]:
             copy.wait()
-        operators[...] = jnp.concatenate([operators_in[kind] for kind in range(types)], axis=1)
+        operators[...] = jnp.zeros_like(operators)
+        for kind in range(types):
+            at = kind * LANES
+            operators[at : at + FACE_DOFS, :FACE_DOFS] = flip(
+                operators_in[kind].astype(F32)
+            ).astype(BF16)
         wanted = flip(links[...].astype(F32)).astype(jnp.int32)
-        fine_gather[...] = gather_matrix(wanted, position, columns * tele, elements)
-        kind_masks(faces[...].astype(F32), fine_kinds, elements)
+        for face, part in enumerate(gather_matrix(wanted, position, columns * tele, elements)):
+            fine_gather[face] = part.astype(BF16)
+        kind_masks(flip(faces[...].astype(F32)).astype(jnp.int32), fine_kinds)
         slabs[place, 0, :coarse_own, :FACES] = coarse_links[...]
         slabs[place, 1, :coarse_own, :FACES] = coarse_faces[...]
         for copy in setup:
@@ -291,7 +287,7 @@
             rows = jnp.concatenate(
                 [rows, jnp.zeros((SLOT - rows.shape[0], DOFS), F32)], axis=0
             )
-        pool[step, SLOT : 2 * SLOT, :] = rows.astype(BF16)
+        pool[step, SLOT : 2 * SLOT, :] = dot(rows.astype(BF16), nodes[...]).astype(BF16)
         copies = [
             pltpu.make_async_remote_copy(
                 src_ref=pool.at[step, pl.ds(SLOT, SLOT)],
@@ -310,30 +306,27 @@
             copy.wait()
         return pool[step]
 
-    def coupling(states, gather, kinds, width):
-        picked = dot(gather[...], states).astype(BF16)
-        traces = dot_nt(trace[...], picked)
-        span = FACES * width
-        lane = lax.broadcasted_iota(jnp.int32, (FACE_DOFS, span), 1)
-        rows = traces[:FACE_DOFS]
-        for face in range(1, FACES):
-            rows = jnp.where(
-                lane >= face * width, traces[face * FACE_DOFS : (face + 1) * FACE_DOFS], rows
-            )
-        rows = rows.astype(BF16)
-        for kind in range(types):
-            masked[kind * FACE_DOFS : (kind + 1) * FACE_DOFS, :span] = rows * kinds[kind]
-        products = dot(operators[...], masked[:, :span]).astype(BF16)
+    def coupling(pool, gather, kinds, width):
+        rows = jnp.concatenate(
+            [
+                dot(gather[face], pool[:, (face ^ 1) * LANES : ((face ^ 1) + 1) * LANES])
+                for face in range(FACES)
+            ],
+            axis=0,
+        ).astype(BF16)
+        masked = jnp.concatenate([rows * kinds[kind] for kind in range(types)], axis=1)
+        products = dot(masked, operators[...])
         stacked = jnp.concatenate(
-            [products[:, face * width : (face + 1) * width] for face in range(FACES)], axis=0
+            [products[face * width : (face + 1) * width] for face in range(FACES)], axis=1
         )
-        return dot(lift[...], stacked)
+        return dot_nt(nodes[...], stacked.astype(BF16))
 
     loads[0].wait()
     right[...] = flip(right_in[...])
     for e in range(elements):
         blocks[e].wait()
         pack(raw, inverse, e)
+    loads[1].wait()
 
     pack_own()
     near_copy.start()
@@ -401,9 +394,9 @@
             kinds = jnp.concatenate(
                 [slabs[t, 1, :coarse_own, :FACES] for t in range(tele)], axis=0
             )
-            kinds = flip(kinds.astype(F32))
-            coarse_gather[...] = gather_matrix(wanted, fine, columns, coarse)
-            kind_masks(kinds, coarse_kinds, coarse)
+            for face, part in enumerate(gather_matrix(wanted, fine, columns, coarse)):
+                coarse_gather[face] = part.astype(BF16)
+            kind_masks(kinds, coarse_kinds)
             near_copy.wait()
             for chunk in range(CHUNKS):
                 chunk_copy(place, chunk, 0, far).wait_send()
@@ -457,7 +450,7 @@
     coarse_own = coarse_inverse.shape[0]
     coarse = coarse_own * tele
     types = face_operators.shape[0]
-    trace, lift = tables()
+    nodes = face_nodes()
     rounds = CYCLES * (SWEEPS + 1)
     coarse_rounds = CYCLES * (SWEEPS - 1)
     vmem = pl.BlockSpec(memory_space=pltpu.VMEM)
@@ -466,7 +459,7 @@
     return pl.pallas_call(
         functools.partial(kernel, tele, fine_size),
         out_shape=jax.ShapeDtypeStruct(right_side.shape, F32),
-        in_specs=[hbm] * 11,
+        in_specs=[hbm] * 10,
         out_specs=vmem,
         scratch_shapes=[
             pltpu.VMEM(fine_inverse.shape, BF16),
@@ -477,21 +470,19 @@
             pltpu.VMEM((FACES, elements), jnp.int32),
             pltpu.VMEM((FACES, elements), jnp.int32),
             pltpu.VMEM(face_operators.shape, BF16),
-            pltpu.VMEM(trace.shape, BF16),
-            pltpu.VMEM(lift.shape, BF16),
+            pltpu.VMEM(nodes.shape, BF16),
             pltpu.VMEM(coarse_links.shape, jnp.int32),
             pltpu.VMEM(coarse_faces.shape, jnp.int32),
             pltpu.SMEM(agglomerate.shape, jnp.int32),
             pltpu.VMEM((coarse, elements), BF16),
             pltpu.VMEM((tele, 2, 8, LANES), jnp.int32),
-            pltpu.VMEM((FACE_DOFS, types * FACE_DOFS), BF16),
-            pltpu.VMEM((types * FACE_DOFS, FACES * elements), BF16),
-            pltpu.VMEM((types, FACE_DOFS, FACES * elements), BF16),
-            pltpu.VMEM((types, FACE_DOFS, FACES * coarse), BF16),
-            pltpu.VMEM((FACES * elements, 3 * SLOT), BF16),
-            pltpu.VMEM((FACES * coarse, 3 * SLOT), BF16),
-            pltpu.VMEM((rounds, 3 * SLOT, DOFS), BF16),
-            pltpu.VMEM((coarse_rounds, 3 * SLOT, DOFS), BF16),
+            pltpu.VMEM((types * LANES, LANES), BF16),
+            pltpu.VMEM((types, FACES * elements, LANES), BF16),
+            pltpu.VMEM((types, FACES * coarse, LANES), BF16),
+            pltpu.VMEM((FACES, elements, 3 * SLOT), BF16),
+            pltpu.VMEM((FACES, coarse, 3 * SLOT), BF16),
+            pltpu.VMEM((rounds, 3 * SLOT, FACES * LANES), BF16),
+            pltpu.VMEM((coarse_rounds, 3 * SLOT, FACES * LANES), BF16),
             pltpu.VMEM((CYCLES, tele, coarse, DOFS), F32),
             pltpu.VMEM((DOFS, elements), F32),
             pltpu.VMEM((DOFS, elements), F32),
@@ -500,7 +491,7 @@
             pltpu.VMEM((DOFS, coarse), F32),
             pltpu.VMEM((DOFS, coarse), F32),
             pltpu.VMEM((DOFS, coarse), F32),
-            dma((9,)),
+            dma((8,)),
             dma((elements,)),
             dma,
             dma,
@@ -530,8 +521,7 @@
         coarse_faces,
         face_operators,
         agglomerate,
-        trace,
-        lift,
+        nodes,
     )
 
 

time: 80.3 us -> 80.7 us (level)
  no operation moved by 1% of the time
where the time goes in v5:
time: 80.7 us; the launch traced here: 80.6 us
  Pallas kernels  79.2 us (98%)
  local copies, waits for them, and re-layouts  1.35 us (2%)
    pallas_call x1, Pallas kernels, shards(): pl.pallas_call(functools.partial(kernel, tele, fine_size), out_shape=jax....  79.2 us

profile of v5, /device:TPU:0, one launch (start us, length us, event | category | flops | bytes accessed | tf_op | source)
XLA Modules:
  0.0 80.6 jit_solution(5771168852359288893)
XLA Ops:
  0.0 79.2 %v_cycles.1 = f32[16,320]{1,0:T(8,128)} custom-call(f32[16,320]{1,0:T(8,128)} %right_hbm.1, bf16[16,320,320]{2,1,0:T(8,128)(2,1)} %inverse_hbm.1, s32[6,16]{1,0:T(8,128)} %bitcast.2, s32[6,16]{1,0:T(8,128)} %bitcast.3, bf16[2,320,320]{2,1,0:T(8,128)(2,1)} %coarse_hbm.1, s32[2,6]{1,0:T(2,128)} %coarse_links_hbm.1, s32[2,6]{1,0:T(2,128)} %coarse_faces_hbm.1, ...), custom_call_target="tpu_custom_call" | custom-call | tf_op jit(solution)/shard_map/v_cycles/pallas_call | solution.py:459
  79.2 1.3 %copy.12 = f32[16,320]{1,0:T(8,128)} copy(f32[16,320]{1,0:T(8,128)} %v_cycles.1) | data formatting | bytes 40960

commit v6 on v4

--- a/solution.py
+++ b/solution.py
@@ -12,7 +12,7 @@
 NODES = 4
 SWEEPS = 3
 CYCLES = 2
-CHUNKS = SWEEPS + 1
+CHUNKS = SWEEPS + 2
 FACES = 6
 FACE_DOFS = FIELDS * NODES * NODES
 DOFS = FIELDS * NODES**3
@@ -170,7 +170,7 @@
         pltpu.make_async_copy(inverse_hbm.at[e], raw.at[e], inverse_sem.at[e])
         for e in range(elements)
     ]
-    for copy in loads[:1] + blocks + [own_block] + loads[1:]:
+    for copy in loads[:1] + [own_block] + blocks + loads[1:]:
         copy.start()
 
     barrier = pltpu.get_barrier_semaphore()
@@ -329,15 +329,16 @@
         )
         return dot(lift[...], stacked)
 
+    pack_own()
+    chunk_copy(place, 0, 0, far).start()
+    chunk_copy(place, 1, 0, far).start()
+    near_copy.start()
+
     loads[0].wait()
     right[...] = flip(right_in[...])
     for e in range(elements):
         blocks[e].wait()
         pack(raw, inverse, e)
-
-    pack_own()
-    near_copy.start()
-    chunk_copy(place, 0, 0, far).start()
 
     @pl.loop(0, CYCLES)
     def cycle_body(cycle):
@@ -360,9 +361,14 @@
 
                 @pl.when(cycle == 0)
                 def pass_on():
-                    chunk_copy(place, s - 1, 0, far).wait_recv()
-                    chunk_copy(far_place, s - 1, 1, near).start()
-                    chunk_copy(place, s, 0, far).start()
+                    @pl.when(s == 1)
+                    def first():
+                        chunk_copy(place, 0, 0, far).wait_recv()
+                        chunk_copy(far_place, 0, 1, near).start()
+
+                    chunk_copy(place, s, 0, far).wait_recv()
+                    chunk_copy(far_place, s, 1, near).start()
+                    chunk_copy(place, s + 1, 0, far).start()
 
                 coupled[...] = coupling(states, fine_gather, fine_kinds, elements)
 

time: 80.3 us -> 81 us (level)
  no operation moved by 1% of the time
where the time goes in v6:
time: 81 us; the launch traced here: 80.8 us
  Pallas kernels  79.4 us (98%)
  local copies, waits for them, and re-layouts  1.35 us (2%)
    pallas_call x1, Pallas kernels, shards(): pl.pallas_call(functools.partial(kernel, tele, fine_size), out_shape=jax....  79.4 us

profile of v6, /device:TPU:0, one launch (start us, length us, event | category | flops | bytes accessed | tf_op | source)
XLA Modules:
  0.0 80.8 jit_solution(17347116554567226448)
XLA Ops:
  0.0 79.4 %v_cycles.1 = f32[16,320]{1,0:T(8,128)} custom-call(f32[16,320]{1,0:T(8,128)} %right_hbm.1, bf16[16,320,320]{2,1,0:T(8,128)(2,1)} %inverse_hbm.1, s32[6,16]{1,0:T(8,128)} %bitcast.2, s32[6,16]{1,0:T(8,128)} %bitcast.3, bf16[2,320,320]{2,1,0:T(8,128)(2,1)} %coarse_hbm.1, s32[2,6]{1,0:T(2,128)} %coarse_links_hbm.1, s32[2,6]{1,0:T(2,128)} %coarse_faces_hbm.1, ...), custom_call_target="tpu_custom_call" | custom-call | tf_op jit(solution)/shard_map/v_cycles/pallas_call | solution.py:472
  79.5 1.3 %copy.13 = f32[16,320]{1,0:T(8,128)} copy(f32[16,320]{1,0:T(8,128)} %v_cycles.1) | data formatting | bytes 40960

commit v7 on v4

--- a/solution.py
+++ b/solution.py
@@ -274,16 +274,31 @@
     def apply_inverse(packed, vectors, width):
         lane = lax.broadcasted_iota(jnp.int32, (1, width), 1)
         alone = [vectors * (lane == e).astype(F32).astype(BF16) for e in range(width)]
-        group = width // len(packed)
-        total = None
-        for i, block in enumerate(packed):
-            own = alone[i * group : (i + 1) * group]
-            spread = jnp.concatenate(
-                [part[:MAIN] for part in own] + [part[MAIN:] for part in own], axis=0
-            )
-            product = dot(block, spread)
-            total = product if total is None else total + product
-        return total
+        spread = [part[:MAIN] for part in alone] + [part[MAIN:] for part in alone]
+        if len(packed.shape) == 2:
+            depth = width * DOFS // 5
+            count = width // 4
+            pieces = [spread[i * count : (i + 1) * count] for i in range(4)] + [spread[width:]]
+            products = [
+                dot(packed[:, i * depth : (i + 1) * depth], jnp.concatenate(piece, axis=0))
+                for i, piece in enumerate(pieces)
+            ]
+        else:
+            group = width // packed.shape[0]
+            products = [
+                dot(
+                    packed[i],
+                    jnp.concatenate(
+                        spread[i * group : (i + 1) * group]
+                        + spread[width + i * group : width + (i + 1) * group],
+                        axis=0,
+                    ),
+                )
+                for i in range(packed.shape[0])
+            ]
+        while len(products) > 1:
+            products = [sum(products[i : i + 2]) for i in range(0, len(products), 2)]
+        return products[0]
 
     def exchange(pool, send, recv, step, partner, value, meanwhile=lambda: None):
         rows = flip(value)
@@ -370,7 +385,7 @@
             def relax():
                 low = (right[...] - coupled[...]).astype(BF16)
                 lowered[...] = low
-                state[...] = apply_inverse([inverse[...]], low, elements)
+                state[...] = apply_inverse(inverse, low, elements)
 
         high, low = split(lowered[...].astype(F32) - coupled[...])
         partials[cycle, 0] = dot_nt(member[...], high) + dot_nt(member[...], low)
@@ -432,7 +447,7 @@
 
             low = restricted[...]
             low = jnp.where(s > 0, low - coarse_coupled[...], low).astype(BF16)
-            coarse_state[...] = apply_inverse([coarse_inverse[t] for t in range(tele)], low, coarse)
+            coarse_state[...] = apply_inverse(coarse_inverse, low, coarse)
 
         high, low = split(coarse_state[...])
         state[...] = state[...] + dot(high, member[...]) + dot(low, member[...])

time: 80.3 us -> 80.3 us (level)
  no operation moved by 1% of the time
where the time goes in v7:
time: 80.3 us; the launch traced here: 80.2 us
  Pallas kernels  78.8 us (98%)
  local copies, waits for them, and re-layouts  1.35 us (2%)
    pallas_call x1, Pallas kernels, shards(): pl.pallas_call(functools.partial(kernel, tele, fine_size), out_shape=jax....  78.8 us

profile of v7, /device:TPU:0, one launch (start us, length us, event | category | flops | bytes accessed | tf_op | source)
XLA Modules:
  0.0 80.2 jit_solution(2655675098050747482)
XLA Ops:
  0.0 78.8 %v_cycles.1 = f32[16,320]{1,0:T(8,128)} custom-call(f32[16,320]{1,0:T(8,128)} %right_hbm.1, bf16[16,320,320]{2,1,0:T(8,128)(2,1)} %inverse_hbm.1, s32[6,16]{1,0:T(8,128)} %bitcast.2, s32[6,16]{1,0:T(8,128)} %bitcast.3, bf16[2,320,320]{2,1,0:T(8,128)(2,1)} %coarse_hbm.1, s32[2,6]{1,0:T(2,128)} %coarse_links_hbm.1, s32[2,6]{1,0:T(2,128)} %coarse_faces_hbm.1, ...), custom_call_target="tpu_custom_call" | custom-call | tf_op jit(solution)/shard_map/v_cycles/pallas_call | solution.py:481
  78.8 1.3 %copy.13 = f32[16,320]{1,0:T(8,128)} copy(f32[16,320]{1,0:T(8,128)} %v_cycles.1) | data formatting | bytes 40960

commit v8 on v4

--- a/solution.py
+++ b/solution.py
@@ -285,14 +285,8 @@
             total = product if total is None else total + product
         return total
 
-    def exchange(pool, send, recv, step, partner, value, meanwhile=lambda: None):
-        rows = flip(value)
-        if rows.shape[0] < SLOT:
-            rows = jnp.concatenate(
-                [rows, jnp.zeros((SLOT - rows.shape[0], DOFS), F32)], axis=0
-            )
-        pool[step, SLOT : 2 * SLOT, :] = rows.astype(BF16)
-        copies = [
+    def sides(pool, send, recv, step, partner):
+        return [
             pltpu.make_async_remote_copy(
                 src_ref=pool.at[step, pl.ds(SLOT, SLOT)],
                 dst_ref=pool.at[step, pl.ds(landing * SLOT, SLOT)],
@@ -303,11 +297,20 @@
             )
             for side, (offset, landing) in enumerate(((1, 0), (-1, 2)))
         ]
+
+    def exchange(pool, send, recv, step, partner, value, meanwhile=lambda: None):
+        rows = flip(value)
+        if rows.shape[0] < SLOT:
+            rows = jnp.concatenate(
+                [rows, jnp.zeros((SLOT - rows.shape[0], DOFS), F32)], axis=0
+            )
+        pool[step, SLOT : 2 * SLOT, :] = rows.astype(BF16)
+        copies = sides(pool, send, recv, step, partner)
         for copy in copies:
             copy.start()
         meanwhile()
         for copy in copies:
-            copy.wait()
+            copy.wait_recv()
         return pool[step]
 
     def coupling(states, gather, kinds, width):
@@ -438,6 +441,12 @@
         state[...] = state[...] + dot(high, member[...]) + dot(low, member[...])
 
     out_ref[...] = flip(state[...])
+    for step in range(1, fine_pool.shape[0]):
+        for copy in sides(fine_pool, fine_send, fine_recv, step, around):
+            copy.wait_send()
+    for step in range(coarse_pool.shape[0]):
+        for copy in sides(coarse_pool, coarse_send, coarse_recv, step, column):
+            copy.wait_send()
 
 
 def shards(

time: 80.3 us -> 80.4 us (level)
  no operation moved by 1% of the time
where the time goes in v8:
time: 80.4 us; the launch traced here: 80.2 us
  Pallas kernels  78.9 us (98%)
  local copies, waits for them, and re-layouts  1.35 us (2%)
    pallas_call x1, Pallas kernels, shards(): pl.pallas_call(functools.partial(kernel, tele, fine_size), out_shape=jax....  78.9 us

profile of v8, /device:TPU:0, one launch (start us, length us, event | category | flops | bytes accessed | tf_op | source)
XLA Modules:
  0.0 80.2 jit_solution(12977844400146802994)
XLA Ops:
  0.0 78.9 %v_cycles.1 = f32[16,320]{1,0:T(8,128)} custom-call(f32[16,320]{1,0:T(8,128)} %right_hbm.1, bf16[16,320,320]{2,1,0:T(8,128)(2,1)} %inverse_hbm.1, s32[6,16]{1,0:T(8,128)} %bitcast.2, s32[6,16]{1,0:T(8,128)} %bitcast.3, bf16[2,320,320]{2,1,0:T(8,128)(2,1)} %coarse_hbm.1, s32[2,6]{1,0:T(2,128)} %coarse_links_hbm.1, s32[2,6]{1,0:T(2,128)} %coarse_faces_hbm.1, ...), custom_call_target="tpu_custom_call" | custom-call | tf_op jit(solution)/shard_map/v_cycles/pallas_call | solution.py:475
  78.9 1.3 %copy.13 = f32[16,320]{1,0:T(8,128)} copy(f32[16,320]{1,0:T(8,128)} %v_cycles.1) | data formatting | bytes 40960
